TPU v7x, 512 devices: a whole 4x8x8 slice. The times are simulated.
512 devices in a mesh: dp: 4 (over z_lo), view: 8 (over x, core), frame: 16 (over z_hi, y).
Axes of the slice: x: 4, y: 8, z: 8 (z_hi: 2, z_lo: 4; z = z_hi * 4 + z_lo), core: 2. Of those that a mesh axis runs over, the one named last changes fastest.
Arguments:
- query_rows: bfloat16 [4, 8, 16, 128, 1024], P('dp', 'view', 'frame'), may hold values from -8 to 8
- key_rows: bfloat16 [4, 8, 16, 128, 1024], P('dp', 'view', 'frame'), may hold values from -8 to 8
- value_rows: bfloat16 [4, 8, 16, 128, 1024], P('dp', 'view', 'frame'), may hold values from -6 to 6
- cotangent: bfloat16 [4, 8, 16, 128, 1024], P('dp', 'view', 'frame'), may hold values from -6 to 6
- out_weight: bfloat16 [1024, 1024], P('frame'), may hold values from -0.1875 to 0.1875
Outputs:
- projected: bfloat16 [4, 8, 16, 128, 1024], P('dp', 'view', 'frame')
- query_grad: bfloat16 [4, 8, 16, 128, 1024], P('dp', 'view', 'frame')
- key_grad: bfloat16 [4, 8, 16, 128, 1024], P('dp', 'view', 'frame')
- value_grad: bfloat16 [4, 8, 16, 128, 1024], P('dp', 'view', 'frame')
- weight_grad: bfloat16 [1024, 1024], P(('view', 'frame'))
All inputs are finite; a program needn't handle non-finite values.
Results may differ from a plain program's by a relative error of at most 0.012.
Values may be sent and summed in bfloat16 or wider, within the bound.
A program may use at most 128 MiB of HBM per device.

v0:
```python
import jax
import jax.numpy as jnp
from jax import lax
from jax.sharding import PartitionSpec as P

HEAD_DIM = 64


def softmax_rows(scores):
    highest = jnp.max(scores, axis=-1, keepdims=True)
    raised = jnp.exp(scores - highest)
    return raised / jnp.sum(raised, axis=-1, keepdims=True)


def to_heads(local_block, length_axis):
    moved_block = jnp.moveaxis(local_block, length_axis, 3)
    heads = moved_block.reshape(
        (-1, moved_block.shape[3], moved_block.shape[4] // HEAD_DIM, HEAD_DIM)
    )
    return (heads, moved_block.shape)


def from_heads(heads, moved_shape, length_axis):
    return jnp.moveaxis(heads.reshape(moved_shape), 3, length_axis)


def score_block(head_queries, head_keys):
    products = jnp.einsum(
        "blhd,bmhd->bhlm", head_queries, head_keys, preferred_element_type=jnp.float32
    )
    return products * HEAD_DIM ** (-0.5)


def attend_forward(query_block, key_block, value_block, length_axis):
    head_queries, moved_shape = to_heads(query_block, length_axis)
    head_keys, moved_shape = to_heads(key_block, length_axis)
    head_values, moved_shape = to_heads(value_block, length_axis)
    probabilities = softmax_rows(score_block(head_queries, head_keys))
    weights = probabilities.astype(jnp.bfloat16)
    mixed_heads = jnp.einsum(
        "bhlm,bmhd->blhd", weights, head_values, preferred_element_type=jnp.float32
    )
    return from_heads(mixed_heads.astype(jnp.bfloat16), moved_shape, length_axis)


def attend_backward(query_block, key_block, value_block, grad_block, length_axis):
    head_queries, moved_shape = to_heads(query_block, length_axis)
    head_keys, moved_shape = to_heads(key_block, length_axis)
    head_values, moved_shape = to_heads(value_block, length_axis)
    head_grad, moved_shape = to_heads(grad_block, length_axis)
    probabilities = softmax_rows(score_block(head_queries, head_keys))
    weights = probabilities.astype(jnp.bfloat16)
    value_part = jnp.einsum(
        "bhlm,blhd->bmhd", weights, head_grad, preferred_element_type=jnp.float32
    ).astype(jnp.bfloat16)
    dprob = jnp.einsum(
        "blhd,bmhd->bhlm", head_grad, head_values, preferred_element_type=jnp.float32
    )
    row_delta = jnp.sum(probabilities * dprob, axis=-1, keepdims=True)
    dscore = (probabilities * (dprob - row_delta)).astype(jnp.bfloat16)
    query_part = jnp.einsum(
        "bhlm,bmhd->blhd", dscore, head_keys, preferred_element_type=jnp.float32
    ) * HEAD_DIM ** (-0.5)
    key_part = jnp.einsum(
        "bhlm,blhd->bmhd", dscore, head_queries, preferred_element_type=jnp.float32
    ) * HEAD_DIM ** (-0.5)
    return (
        from_heads(query_part.astype(jnp.bfloat16), moved_shape, length_axis),
        from_heads(key_part.astype(jnp.bfloat16), moved_shape, length_axis),
        from_heads(value_part, moved_shape, length_axis),
    )


def summed(pieces):
    running_total = pieces[0].astype(jnp.float32)
    for piece_part in pieces[1:]:
        running_total = running_total + piece_part.astype(jnp.float32)
    return running_total.astype(jnp.bfloat16)


def local(query_rows, key_rows, value_rows, cotangent, out_weight):
    full_weight = lax.all_gather(out_weight, "frame", axis=0, tiled=True)
    spatial_out = attend_forward(query_rows, key_rows, value_rows, 3)
    view_queries, view_keys, view_values = (
        lax.all_to_all(query_rows, "view", split_axis=3, concat_axis=1, tiled=True),
        lax.all_to_all(key_rows, "view", split_axis=3, concat_axis=1, tiled=True),
        lax.all_to_all(value_rows, "view", split_axis=3, concat_axis=1, tiled=True),
    )
    frame_queries, frame_keys, frame_values = (
        lax.all_to_all(query_rows, "frame", split_axis=3, concat_axis=2, tiled=True),
        lax.all_to_all(key_rows, "frame", split_axis=3, concat_axis=2, tiled=True),
        lax.all_to_all(value_rows, "frame", split_axis=3, concat_axis=2, tiled=True),
    )
    view_local = attend_forward(view_queries, view_keys, view_values, 1)
    frame_local = attend_forward(frame_queries, frame_keys, frame_values, 2)
    view_out = lax.all_to_all(view_local, "view", split_axis=1, concat_axis=3, tiled=True)
    frame_out = lax.all_to_all(frame_local, "frame", split_axis=2, concat_axis=3, tiled=True)
    attended = summed((spatial_out, view_out, frame_out))
    model_width = full_weight.shape[0]
    flat_attended = attended.reshape((-1, model_width))
    flat_grad = cotangent.reshape((-1, model_width))
    projected = (
        jnp.dot(flat_attended, full_weight, preferred_element_type=jnp.float32)
        .astype(jnp.bfloat16)
        .reshape(attended.shape)
    )
    grad_float = lax.dot_general(
        flat_grad, full_weight, (((1,), (1,)), ((), ())), preferred_element_type=jnp.float32
    )
    grad_attended = grad_float.astype(jnp.bfloat16).reshape(attended.shape)
    sample_count = lax.axis_size("dp")
    group_count = lax.axis_size("view") * lax.axis_size("frame")
    token_total = flat_attended.shape[0] * sample_count * group_count
    grad_scale = token_total ** (-0.5)
    shares = lax.psum_scatter(
        lax.dot_general(
            flat_attended, flat_grad, (((0,), (0,)), ((), ())), preferred_element_type=jnp.float32
        ),
        ("view", "frame"),
        scatter_dimension=0,
        tiled=True,
    )
    weight_grad = (lax.psum(shares, "dp") * grad_scale).astype(jnp.bfloat16)
    spatial_grads = attend_backward(query_rows, key_rows, value_rows, grad_attended, 3)
    view_grad_in = lax.all_to_all(grad_attended, "view", split_axis=3, concat_axis=1, tiled=True)
    frame_grad_in = lax.all_to_all(grad_attended, "frame", split_axis=3, concat_axis=2, tiled=True)
    view_query, view_key, view_value = attend_backward(
        view_queries, view_keys, view_values, view_grad_in, 1
    )
    frame_query, frame_key, frame_value = attend_backward(
        frame_queries, frame_keys, frame_values, frame_grad_in, 2
    )
    view_grads = (
        lax.all_to_all(view_query, "view", split_axis=1, concat_axis=3, tiled=True),
        lax.all_to_all(view_key, "view", split_axis=1, concat_axis=3, tiled=True),
        lax.all_to_all(view_value, "view", split_axis=1, concat_axis=3, tiled=True),
    )
    frame_grads = (
        lax.all_to_all(frame_query, "frame", split_axis=2, concat_axis=3, tiled=True),
        lax.all_to_all(frame_key, "frame", split_axis=2, concat_axis=3, tiled=True),
        lax.all_to_all(frame_value, "frame", split_axis=2, concat_axis=3, tiled=True),
    )
    query_grad = summed((spatial_grads[0], view_grads[0], frame_grads[0]))
    key_grad = summed((spatial_grads[1], view_grads[1], frame_grads[1]))
    value_grad = summed((spatial_grads[2], view_grads[2], frame_grads[2]))
    return (projected, query_grad, key_grad, value_grad, weight_grad)


def solution(mesh):
    in_specs = (
        P("dp", "view", "frame", None, None),
        P("dp", "view", "frame", None, None),
        P("dp", "view", "frame", None, None),
        P("dp", "view", "frame", None, None),
        P("frame", None),
    )
    out_specs = (
        P("dp", "view", "frame", None, None),
        P("dp", "view", "frame", None, None),
        P("dp", "view", "frame", None, None),
        P("dp", "view", "frame", None, None),
        P(("view", "frame"), None),
    )
    return jax.shard_map(local, mesh=mesh, in_specs=in_specs, out_specs=out_specs, check_vma=False)
```

profile of v0, /device:TPU:64, one launch (start us, length us, event | category | flops | bytes accessed | tf_op | source)
XLA Modules:
  0.0 1002.3 jit_solution(9602728422197246047)
XLA Ops:
  13.0 4.3 all-to-all-start.2
  21.6 3.3 all-to-all-done.2
  24.8 3.4 all-to-all-start.1
  31.7 4.0 all-to-all-done.1
  35.7 3.4 all-to-all-start
  42.6 4.0 all-to-all-done
  46.6 15.0 %all-to-all-start.6 = ((bf16[16,2,4096]{2,1,0:T(2,128)(2,1)}), bf16[16,2,4096]{2,1,0:T(2,128)(2,1)S(1)}, u32[]{:S(2)}, u32[]{:S(2)}) async-start(bf16[16,2,4096]{2,1,0:T(2,128)(2,1)} %reshape.484), calls=%async_computation.6 | async-start | bytes 524288 | tf_op jit(solution)/shard_map/all_to_all | solution.py:92
  65.0 10.4 %all-to-all-done.6 = bf16[16,2,4096]{2,1,0:T(2,128)(2,1)S(1)} async-done(((bf16[16,2,4096]{2,1,0:T(2,128)(2,1)}), bf16[16,2,4096]{2,1,0:T(2,128)(2,1)S(1)}, u32[]{:S(2)}, u32[]{:S(2)}) %all-to-all-start.6) | async-done | bytes 262176 | tf_op jit(solution)/shard_map/all_to_all | solution.py:92
  75.4 5.0 all-to-all-start.5
  88.1 7.4 all-to-all-done.5
  95.5 4.7 all-to-all-start.4
  107.7 6.3 all-to-all-done.4
  114.1 3.8 all-to-all-start.3
  125.3 5.8 all-to-all-start.7
  134.3 11.6 %all-to-all-done.7 = bf16[1,1,16,8,1024]{4,3,1,0,2:T(8,128)(2,1)S(1)} async-done(((bf16[1,1,16,8,1024]{4,3,1,0,2:T(8,128)(2,1)}), bf16[1,1,16,8,1024]{4,3,1,0,2:T(8,128)(2,1)S(1)}, u32[]{:S(2)}, u32[]{:S(2)}) %all-to-all-start.7) | async-done | bytes 262176 | tf_op jit(solution)/shard_map/all_to_all | solution.py:97
  165.7 3.7 all-to-all-start.8
  177.0 5.3 all-to-all-start.10
  196.4 3.4 all-to-all-start.9
  200.6 3.4 multiply_reduce_fusion
  204.0 3.3 all-to-all-done.9
  207.3 3.4 all-to-all-start.12
  212.5 5.8 all-to-all-done.12
  218.3 3.4 all-to-all-start.14
  223.6 5.6 all-to-all-done.14
  229.2 9.0 all-to-all-start.11
  241.8 10.2 %all-to-all-done.11 = bf16[1,1,16,8,1024]{4,3,1,0,2:T(8,128)(2,1)} async-done(((bf16[1,1,16,8,1024]{4,3,1,0,2:T(8,128)(2,1)}), bf16[1,1,16,8,1024]{4,3,1,0,2:T(8,128)(2,1)}, u32[]{:S(2)}, u32[]{:S(2)}) %all-to-all-start.11) | async-done | bytes 262176 | tf_op jit(solution)/shard_map/all_to_all | solution.py:139
  252.0 4.9 all-to-all-start.13
  261.1 9.7 all-to-all-done.13
  270.7 4.8 all-to-all-start.15
  279.1 10.3 %all-to-all-done.15 = bf16[1,1,16,8,1024]{4,3,1,0,2:T(8,128)(2,1)S(1)} async-done(((bf16[1,1,16,8,1024]{4,3,1,0,2:T(8,128)(2,1)}), bf16[1,1,16,8,1024]{4,3,1,0,2:T(8,128)(2,1)S(1)}, u32[]{:S(2)}, u32[]{:S(2)}) %all-to-all-start.15) | async-done | bytes 262176 | tf_op jit(solution)/shard_map/all_to_all | solution.py:141
  290.2 688.5 %reduce-scatter.2.cloned.1.call-done = f32[8,1024]{1,0:T(8,128)} async-done(((f32[1024,1024]{1,0:T(8,128)}), f32[8,1024]{1,0:T(8,128)}) %reduce-scatter.2.cloned.1.call-update) | async-done | bytes 32784 | tf_op jit(solution)/shard_map/reduce_scatter | solution.py:115
  978.7 15.2 %psum.7 = f32[8,1024]{1,0:T(8,128)S(1)} all-reduce(f32[8,1024]{1,0:T(8,128)} %reduce-scatter.2.cloned.1.call-done), channel_id=1, replica_groups=mesh['dp'=4,'view'=8,'frame'=16] {'dp'}, use_global_device_ids=true, to_apply=%region_10.0 | all-reduce | flops 8192 | bytes 65536 | tf_op jit(solution)/shard_map/psum | solution.py:123
  (195 shorter events, 102.9 us)
Async XLA Ops:
  8.0 143.4 %copy-start = (bf16[1,1,1,128,1024]{4,3,2,1,0:T(8,128)(2,1)S(1)}, bf16[1,1,1,128,1024]{4,3,2,1,0:T(8,128)(2,1)}, u32[]{:S(2)}) copy-start(bf16[1,1,1,128,1024]{4,3,2,1,0:T(8,128)(2,1)} %param.8) | copy-start | bytes 786436
  12.1 16.2 %copy-start.3 = (bf16[1,1,1,128,1024]{4,3,2,1,0:T(8,128)(2,1)S(1)}, bf16[1,1,1,128,1024]{4,3,2,1,0:T(8,128)(2,1)}, u32[]{:S(2)}) copy-start(bf16[1,1,1,128,1024]{4,3,2,1,0:T(8,128)(2,1)} %param.5) | copy-start | bytes 786436
  13.0 11.8 %all-to-all-start.2 = ((bf16[8,2,8192]{2,1,0:T(2,128)(2,1)}), bf16[8,2,8192]{2,1,0:T(2,128)(2,1)S(1)}, u32[]{:S(2)}, u32[]{:S(2)}) async-start(bf16[8,2,8192]{2,1,0:T(2,128)(2,1)} %reshape.478), calls=%async_computation.2 | async-start | bytes 524288 | tf_op jit(solution)/shard_map/all_to_all | solution.py:87
  17.3 137.8 %all-gather.2.cloned.1.call-start = ((), (), s32[]{:S(2)}) async-start(), calls=%async_computation.17 | async-start | bytes 2228224 | tf_op jit(solution)/shard_map/all_gather | solution.py:82
  18.5 20.7 %copy-start.2 = (bf16[1,1,1,128,1024]{4,3,2,1,0:T(8,128)(2,1)S(1)}, bf16[1,1,1,128,1024]{4,3,2,1,0:T(8,128)(2,1)}, u32[]{:S(2)}) copy-start(bf16[1,1,1,128,1024]{4,3,2,1,0:T(8,128)(2,1)} %param.7) | copy-start | bytes 786436
  24.8 10.9 %all-to-all-start.1 = ((bf16[8,2,8192]{2,1,0:T(2,128)(2,1)}), bf16[8,2,8192]{2,1,0:T(2,128)(2,1)S(1)}, u32[]{:S(2)}, u32[]{:S(2)}) async-start(bf16[8,2,8192]{2,1,0:T(2,128)(2,1)} %reshape.480), calls=%async_computation.1 | async-start | bytes 524288 | tf_op jit(solution)/shard_map/all_to_all | solution.py:86
  35.7 10.9 %all-to-all-start = ((bf16[8,2,8192]{2,1,0:T(2,128)(2,1)}), bf16[8,2,8192]{2,1,0:T(2,128)(2,1)S(1)}, u32[]{:S(2)}, u32[]{:S(2)}) async-start(bf16[8,2,8192]{2,1,0:T(2,128)(2,1)} %reshape.482), calls=%async_computation | async-start | bytes 524288 | tf_op jit(solution)/shard_map/all_to_all | solution.py:85
  46.6 28.8 %all-to-all-start.6 = ((bf16[16,2,4096]{2,1,0:T(2,128)(2,1)}), bf16[16,2,4096]{2,1,0:T(2,128)(2,1)S(1)}, u32[]{:S(2)}, u32[]{:S(2)}) async-start(bf16[16,2,4096]{2,1,0:T(2,128)(2,1)} %reshape.484), calls=%async_computation.6 | async-start | bytes 524288 | tf_op jit(solution)/shard_map/all_to_all | solution.py:92
  75.4 20.1 %all-to-all-start.5 = ((bf16[16,2,4096]{2,1,0:T(2,128)(2,1)}), bf16[16,2,4096]{2,1,0:T(2,128)(2,1)S(1)}, u32[]{:S(2)}, u32[]{:S(2)}) async-start(bf16[16,2,4096]{2,1,0:T(2,128)(2,1)} %reshape.486), calls=%async_computation.5 | async-start | bytes 524288 | tf_op jit(solution)/shard_map/all_to_all | solution.py:91
  81.8 67.5 %copy-start.12 = (bf16[1,1,1,128,1024]{3,4,2,1,0:T(8,128)(2,1)}, bf16[1,1,1,128,1024]{3,4,2,1,0:T(8,128)(2,1)S(1)}, u32[]{:S(2)}) copy-start(bf16[1,1,1,128,1024]{3,4,2,1,0:T(8,128)(2,1)S(1)} %copy.217) | copy-start | bytes 786436
  82.0 49.2 %copy-start.14 = (bf16[1,1,1,128,1024]{3,4,2,1,0:T(8,128)(2,1)}, bf16[1,1,1,128,1024]{3,4,2,1,0:T(8,128)(2,1)S(1)}, u32[]{:S(2)}) copy-start(bf16[1,1,1,128,1024]{3,4,2,1,0:T(8,128)(2,1)S(1)} %copy.218) | copy-start | bytes 786436
  95.5 18.6 %all-to-all-start.4 = ((bf16[16,2,4096]{2,1,0:T(2,128)(2,1)}), bf16[16,2,4096]{2,1,0:T(2,128)(2,1)S(1)}, u32[]{:S(2)}, u32[]{:S(2)}) async-start(bf16[16,2,4096]{2,1,0:T(2,128)(2,1)} %reshape.488), calls=%async_computation.4 | async-start | bytes 524288 | tf_op jit(solution)/shard_map/all_to_all | solution.py:90
  114.1 11.3 %all-to-all-start.3 = ((bf16[1,8,1,16,1024]{4,3,2,0,1:T(8,128)(2,1)}), bf16[1,8,1,16,1024]{4,3,2,0,1:T(8,128)(2,1)S(1)}, u32[]{:S(2)}, u32[]{:S(2)}) async-start(bf16[1,8,1,16,1024]{4,3,2,0,1:T(8,128)(2,1)} %copy.232), calls=%async_computation.3 | async-start | bytes 524288 | tf_op jit(solution)/shard_map/all_to_all | solution.py:96
  125.3 20.6 %all-to-all-start.7 = ((bf16[1,1,16,8,1024]{4,3,1,0,2:T(8,128)(2,1)}), bf16[1,1,16,8,1024]{4,3,1,0,2:T(8,128)(2,1)S(1)}, u32[]{:S(2)}, u32[]{:S(2)}) async-start(bf16[1,1,16,8,1024]{4,3,1,0,2:T(8,128)(2,1)} %copy.246), calls=%async_computation.7 | async-start | bytes 524288 | tf_op jit(solution)/shard_map/all_to_all | solution.py:97
  131.2 847.6 %reduce-scatter.2.cloned.1.call-start = ((), (), s32[]{:S(2)}) async-start(), calls=%async_computation.18 | async-start | bytes 4227072 | tf_op jit(solution)/shard_map/reduce_scatter | solution.py:115
  165.7 11.4 %all-to-all-start.8 = ((bf16[8,2,8192]{2,1,0:T(2,128)(2,1)}), bf16[8,2,8192]{2,1,0:T(2,128)(2,1)S(1)}, u32[]{:S(2)}, u32[]{:S(2)}) async-start(bf16[8,2,8192]{2,1,0:T(2,128)(2,1)} %reshape.490), calls=%async_computation.8 | async-start | bytes 524288 | tf_op jit(solution)/shard_map/all_to_all | solution.py:125
  177.0 19.4 %all-to-all-start.10 = ((bf16[16,2,4096]{2,1,0:T(2,128)(2,1)}), bf16[16,2,4096]{2,1,0:T(2,128)(2,1)S(1)}, u32[]{:S(2)}, u32[]{:S(2)}) async-start(bf16[16,2,4096]{2,1,0:T(2,128)(2,1)} %reshape.492), calls=%async_computation.10 | async-start | bytes 524288 | tf_op jit(solution)/shard_map/all_to_all | solution.py:126
  196.4 10.9 %all-to-all-start.9 = ((bf16[1,8,1,16,1024]{4,3,2,0,1:T(8,128)(2,1)}), bf16[1,8,1,16,1024]{4,3,2,0,1:T(8,128)(2,1)S(1)}, u32[]{:S(2)}, u32[]{:S(2)}) async-start(bf16[1,8,1,16,1024]{4,3,2,0,1:T(8,128)(2,1)} %copy.257), calls=%async_computation.9 | async-start | bytes 524288 | tf_op jit(solution)/shard_map/all_to_all | solution.py:134
  204.0 17.7 %copy-start.6 = (bf16[8,16,16,64]{3,2,0,1:T(8,128)(2,1)S(1)}, bf16[8,16,16,64]{3,2,0,1:T(8,128)(2,1)}, u32[]{:S(2)}) copy-start(bf16[8,16,16,64]{3,2,0,1:T(8,128)(2,1)} %copy-done.5) | copy-start | bytes 786436
  207.3 11.0 %all-to-all-start.12 = ((bf16[1,8,1,16,1024]{4,3,2,0,1:T(8,128)(2,1)}), bf16[1,8,1,16,1024]{4,3,2,0,1:T(8,128)(2,1)S(1)}, u32[]{:S(2)}, u32[]{:S(2)}) async-start(bf16[1,8,1,16,1024]{4,3,2,0,1:T(8,128)(2,1)} %copy.272), calls=%async_computation.12 | async-start | bytes 524288 | tf_op jit(solution)/shard_map/all_to_all | solution.py:135
  218.3 10.9 %all-to-all-start.14 = ((bf16[1,8,1,16,1024]{4,3,2,0,1:T(8,128)(2,1)}), bf16[1,8,1,16,1024]{4,3,2,0,1:T(8,128)(2,1)S(1)}, u32[]{:S(2)}, u32[]{:S(2)}) async-start(bf16[1,8,1,16,1024]{4,3,2,0,1:T(8,128)(2,1)} %copy.282), calls=%async_computation.14 | async-start | bytes 524288 | tf_op jit(solution)/shard_map/all_to_all | solution.py:136
  221.8 16.4 %copy-start.16 = (bf16[1,1,1,128,1024]{3,4,2,1,0:T(8,128)(2,1)S(1)}, bf16[1,1,1,128,1024]{3,4,2,1,0:T(8,128)(2,1)}, u32[]{:S(2)}) copy-start(bf16[1,1,1,128,1024]{3,4,2,1,0:T(8,128)(2,1)} %copy-done.14) | copy-start | bytes 786436
  221.8 16.4 %copy-start.32 = (bf16[128,1024]{0,1:T(8,128)(2,1)S(1)}, bf16[128,1024]{0,1:T(8,128)(2,1)}, u32[]{:S(2)}) copy-start(bf16[128,1024]{0,1:T(8,128)(2,1)} %copy-done.31) | copy-start | bytes 786436
  229.2 22.8 %all-to-all-start.11 = ((bf16[1,1,16,8,1024]{4,3,1,0,2:T(8,128)(2,1)}), bf16[1,1,16,8,1024]{4,3,1,0,2:T(8,128)(2,1)}, u32[]{:S(2)}, u32[]{:S(2)}) async-start(bf16[1,1,16,8,1024]{4,3,1,0,2:T(8,128)(2,1)} %copy.267), calls=%async_computation.11 | async-start | bytes 524288 | tf_op jit(solution)/shard_map/all_to_all | solution.py:139
  240.0 17.0 %copy-start.1 = (bf16[1024,1024]{1,0:T(8,128)(2,1)S(1)}, bf16[1024,1024]{1,0:T(8,128)(2,1)}, u32[]{:S(2)}) copy-start(bf16[1024,1024]{1,0:T(8,128)(2,1)} %all-gather.2.cloned.1.call-done) | copy-start | bytes 6291460
  241.8 17.3 %copy-start.23 = (f32[8,16,16,16]{2,3,1,0:T(8,128)S(1)}, f32[8,16,16,16]{2,3,1,0:T(8,128)}, u32[]{:S(2)}) copy-start(f32[8,16,16,16]{2,3,1,0:T(8,128)} %get-tuple-element.10) | copy-start | bytes 393220
  252.0 18.7 %all-to-all-start.13 = ((bf16[1,1,16,8,1024]{4,3,1,0,2:T(8,128)(2,1)}), bf16[1,1,16,8,1024]{4,3,1,0,2:T(8,128)(2,1)}, u32[]{:S(2)}, u32[]{:S(2)}) async-start(bf16[1,1,16,8,1024]{4,3,1,0,2:T(8,128)(2,1)} %copy.277), calls=%async_computation.13 | async-start | bytes 524288 | tf_op jit(solution)/shard_map/all_to_all | solution.py:140
  259.7 17.7 %copy-start.10 = (f32[1,1,1,128,1024]{4,3,2,1,0:T(8,128)S(1)}, f32[1,1,1,128,1024]{4,3,2,1,0:T(8,128)}, u32[]{:S(2)}) copy-start(f32[1,1,1,128,1024]{4,3,2,1,0:T(8,128)} %copy.274) | copy-start | bytes 1572868
  259.7 17.6 %copy-start.20 = (bf16[1,8,1,16,1024]{4,3,2,0,1:T(8,128)(2,1)S(1)}, bf16[1,8,1,16,1024]{4,3,2,0,1:T(8,128)(2,1)}, u32[]{:S(2)}) copy-start(bf16[1,8,1,16,1024]{4,3,2,0,1:T(8,128)(2,1)} %copy-done.19) | copy-start | bytes 786436
  259.8 29.6 %copy-start.11 = (f32[1,1,1,128,1024]{4,3,2,1,0:T(8,128)S(1)}, f32[1,1,1,128,1024]{4,3,2,1,0:T(8,128)}, u32[]{:S(2)}) copy-start(f32[1,1,1,128,1024]{4,3,2,1,0:T(8,128)} %copy.284) | copy-start | bytes 1572868
  259.9 29.6 %copy-start.22 = (bf16[1,8,1,16,1024]{4,3,2,0,1:T(8,128)(2,1)S(1)}, bf16[1,8,1,16,1024]{4,3,2,0,1:T(8,128)(2,1)}, u32[]{:S(2)}) copy-start(bf16[1,8,1,16,1024]{4,3,2,0,1:T(8,128)(2,1)} %copy-done.21) | copy-start | bytes 786436
  270.7 18.7 %all-to-all-start.15 = ((bf16[1,1,16,8,1024]{4,3,1,0,2:T(8,128)(2,1)}), bf16[1,1,16,8,1024]{4,3,1,0,2:T(8,128)(2,1)S(1)}, u32[]{:S(2)}, u32[]{:S(2)}) async-start(bf16[1,1,16,8,1024]{4,3,1,0,2:T(8,128)(2,1)} %copy.287), calls=%async_computation.15 | async-start | bytes 524288 | tf_op jit(solution)/shard_map/all_to_all | solution.py:141
  (22 other events, 152.1 us)
Sparse Core Ops, SparseCore 0:
  21.3 123.4 all-gather.1
Sparse Core Ops, SparseCore 1:
  154.2 824.5 reduce-scatter.1
where the time goes:
time: 1010 us; the launch traced here: 1000 us
  waiting for transfers between devices  789 us (78%)
  starting transfers between devices  83.5 us (8%)
  local copies, waits for them, and re-layouts  39.7 us (4%)
  matrix products  31.8 us (3%)
  other arithmetic  26.2 us (3%)
  between operations  16.8 us (2%)
  blocking collectives  15.2 us (2%)
    reduce_scatter x1, waiting for transfers between devices, local(): lax.psum_scatter(lax.dot_general(flat_attended, flat_grad, (((0,), (0,)),...  689 us
  transfers between devices with their start and end apart: 18, of which 17 were waited for; matrix products, arithmetic and copies ran while one was open for 9% of the time, Pallas kernels for 0%

commit v1 on v0

v1 whole, which is shorter than its diff:
```python
import functools

import jax
import jax.numpy as jnp
from jax import lax
from jax.experimental import pallas as pl
from jax.experimental.pallas import tpu as pltpu
from jax.sharding import PartitionSpec as P

F32 = jnp.float32
BF16 = jnp.bfloat16
MESH = pl.DeviceIdType.MESH
NN = (((1,), (0,)), ((), ()))
NT = (((1,), (1,)), ((), ()))
TN = (((0,), (0,)), ((), ()))
MASKED = -1e30

D = 1024
VIEWS = 8
FRAMES = 16
CHIPS = VIEWS // 2
PAIRS = D // 128
HALF = D // 2
SCALE = 0.125


def dot(left, right, dims):
    return lax.dot_general(left, right, dims, preferred_element_type=F32)


def flat(block):
    return block.reshape(block.shape[0] * block.shape[1], block.shape[2])


def blocks(rows):
    return rows.reshape(rows.shape[0] // 8, 8, rows.shape[1])


def lower_lanes():
    return lax.broadcasted_iota(jnp.int32, (128, 128), 1) < 64


def by_head(rows, lower):
    one = lower.astype(F32).astype(BF16)
    other = (1.0 - lower.astype(F32)).astype(BF16)
    return jnp.concatenate([rows * one, rows * other], axis=0)


def group_bias(modulus):
    row = lax.broadcasted_iota(jnp.int32, (128, 128), 0)
    column = lax.broadcasted_iota(jnp.int32, (128, 128), 1)
    same = lax.rem(row, modulus) == lax.rem(column, modulus)
    return jnp.where(same, 0.0, MASKED).astype(F32)


def forward_pair(query, key, value, bias, lower):
    scores = dot(by_head(key, lower), query, NT) * SCALE
    halves = []
    for head in range(2):
        part = scores[128 * head : 128 * head + 128]
        if bias is not None:
            part = part + bias
        raised = jnp.exp(part - jnp.max(part, axis=0, keepdims=True))
        halves.append(raised * (1.0 / jnp.sum(raised, axis=0, keepdims=True)))
    probs = jnp.concatenate(halves, axis=0)
    out = dot(probs.astype(BF16), by_head(value, lower), TN)
    return probs, out


def backward_pair(query, key, value, grad, probs, lower):
    dprob = dot(by_head(value, lower), grad, NT)
    halves = []
    for head in range(2):
        prob = probs[128 * head : 128 * head + 128]
        term = prob * dprob[128 * head : 128 * head + 128]
        halves.append((term - prob * jnp.sum(term, axis=0, keepdims=True)).astype(BF16))
    dscore = jnp.concatenate(halves, axis=0)
    value_grad = dot(probs.astype(BF16), grad, NN)
    value_grad = jnp.where(lower, value_grad[:128], value_grad[128:])
    key_grad = dot(dscore, query, NN)
    key_grad = jnp.where(lower, key_grad[:128], key_grad[128:]) * SCALE
    query_grad = dot(dscore, by_head(key, lower), TN) * SCALE
    return query_grad, key_grad, value_grad


def frame_offset(step):
    far = lax.rem(step, 2)
    turn = step // 2
    odd = lax.rem(turn, 2)
    near = odd * ((turn + 1) // 2) + (1 - odd) * lax.rem(8 - turn // 2, 8)
    return near, far


def kernel(
    q_hbm, k_hbm, v_hbm, c_hbm, w_hbm,
    proj_hbm, dq_hbm, dk_hbm, dv_hbm, wg_hbm,
    own, of_view, of_frame, shard, weight,
    own_res, view_res, frame_res, view_back, frame_back,
    own_probs, view_probs, grad, rows,
    core_out, core_in, chip_out, chip_in, frame_out, frame_in, sample_out, sample_in,
    results, last,
    load_sem, store_sem, send_sem, recv_sem, core_send, core_recv, chip_send, chip_recv,
    slice_send, slice_recv, pass_send, pass_recv,
):
    sample = lax.axis_index("dp")
    view = lax.axis_index("view")
    frame = lax.axis_index("frame")
    chip = view // 2
    core = lax.rem(view, 2)
    far = frame // 8
    near = lax.rem(frame, 8)
    partner = {"view": chip * 2 + 1 - core}

    def frame_peer(step):
        by, across = frame_offset(step)
        return lax.rem(far + across, 2) * 8 + lax.rem(near + by, 8)

    def view_peer(step):
        return lax.rem(view + step, VIEWS)

    def sample_peer(step):
        return lax.rem(sample + step, 4)

    def chip_peer(step):
        return lax.rem(chip + step, CHIPS)

    def chip_device(step):
        return {"view": chip_peer(step) * 2 + core}

    def remote(source, target, send, recv, device):
        return pltpu.make_async_remote_copy(
            src_ref=source, dst_ref=target, send_sem=send, recv_sem=recv,
            device_id=device, device_id_type=MESH,
        )

    def each(first, last_step, body):
        def step(index, carry):
            body(index)
            return carry

        lax.fori_loop(first, last_step, step, 0)

    loads = [pltpu.make_async_copy(w_hbm, shard, load_sem.at[4])]
    for index, source in enumerate((q_hbm, k_hbm, v_hbm, c_hbm)):
        loads.append(pltpu.make_async_copy(source, own.at[index], load_sem.at[index]))
    for load in loads:
        load.start()
    barrier = pltpu.get_barrier_semaphore()

    def greet(device):
        pl.semaphore_signal(barrier, inc=1, device_id=device, device_id_type=MESH)

    each(1, FRAMES, lambda step: greet({"frame": frame_peer(step)}))
    each(1, VIEWS, lambda step: greet({"view": view_peer(step)}))
    each(1, 4, lambda step: greet({"dp": sample_peer(step)}))
    pl.semaphore_wait(barrier, FRAMES - 1 + VIEWS - 1 + 3)

    columns = pl.ds(pl.multiple_of(view * 128, 128), 128)
    shard_rows = pl.ds(pl.multiple_of(frame * 64, 64), 64)
    loads[0].wait()

    def send_weight(step):
        remote(
            shard.at[:, columns], weight.at[shard_rows, columns], send_sem.at[0], recv_sem.at[0],
            {"frame": frame_peer(step)},
        ).start()

    each(1, FRAMES, send_weight)
    for load in loads[1:]:
        load.wait()

    def send_view(step):
        peer = view_peer(step)
        remote(
            own.at[:, pl.ds(peer * 2, 2)], of_view.at[:, pl.ds(view * 2, 2)], send_sem.at[1], recv_sem.at[1],
            {"view": peer},
        ).start()

    def send_frame_grad(step):
        peer = frame_peer(step)
        remote(own.at[3, peer], of_frame.at[3, frame], send_sem.at[2], recv_sem.at[2], {"frame": peer}).start()

    def send_frame_rows(half):
        lanes = pl.ds(half * HALF, HALF)

        def send(step):
            peer = frame_peer(step)
            remote(
                own.at[pl.ds(0, 3), peer, :, lanes], of_frame.at[pl.ds(0, 3), frame, :, lanes],
                send_sem.at[3 + half], recv_sem.at[3 + half], {"frame": peer},
            ).start()

        return send

    each(1, VIEWS, send_view)
    each(1, FRAMES, send_frame_grad)
    each(1, FRAMES, send_frame_rows(0))
    each(1, FRAMES, send_frame_rows(1))

    weight[shard_rows, columns] = shard[:, columns]
    of_frame[:, pl.ds(frame, 1)] = own[:, pl.ds(frame, 1)]
    of_view[:, pl.ds(view * 2, 2)] = own[:, pl.ds(view * 2, 2)]

    lower = lower_lanes()

    def lanes_of(pair):
        return pl.ds(pl.multiple_of(pair * 128, 128), 128)

    def forward(source, target, kept, bias):
        def step(pair):
            lanes = lanes_of(pair)
            query, key, value = (flat(source[index, :, :, lanes]) for index in range(3))
            probs, out = forward_pair(query, key, value, bias, lower)
            kept[pair] = probs
            target[0, :, :, lanes] = blocks(out.astype(BF16))

        def two(index):
            step(index * 2)
            step(index * 2 + 1)

        each(0, PAIRS // 2, two)

    def grad_rows(source):
        cotangent = flat(source[3])
        for part in range(4):
            wide = slice(256 * part, 256 * part + 256)
            grad[:, wide] = dot(cotangent, weight[wide, :], NT).astype(BF16)

    def backward_step(source, target, probs, pair):
        lanes = lanes_of(pair)
        query, key, value = (flat(source[index, :, :, lanes]) for index in range(3))
        grads = backward_pair(query, key, value, grad[:, lanes], probs, lower)
        for index, term in enumerate(grads):
            target[1 + index, :, :, lanes] = blocks(term.astype(BF16))

    def backward(source, target, kept):
        grad_rows(source)

        def two(index):
            for pair in (index * 2, index * 2 + 1):
                backward_step(source, target, kept[pair], pair)

        each(0, PAIRS // 2, two)

    forward(own, own_res, own_probs, None)

    gathered = remote(
        weight.at[pl.ds(0, 64 * (FRAMES - 1)), columns], weight.at[pl.ds(0, 64 * (FRAMES - 1)), columns],
        send_sem.at[0], recv_sem.at[0], partner,
    )
    gathered.wait_recv()
    slices = []
    for step in (1, 3, 2):
        slices.append(
            remote(
                weight.at[:, columns], weight.at[:, columns], slice_send.at[step], slice_recv.at[step],
                chip_device(step),
            )
        )
    passes = [remote(weight.at[:, columns], weight.at[:, columns], pass_send.at[0], pass_recv.at[0], partner)]
    for copy in slices + passes:
        copy.start()

    view_bytes = remote(
        own.at[:, pl.ds(0, 2 * (VIEWS - 1))], of_view.at[:, pl.ds(0, 2 * (VIEWS - 1))], send_sem.at[1],
        recv_sem.at[1], partner,
    )
    view_bytes.wait_recv()
    forward(of_view, view_res, view_probs, group_bias(16))

    for copy, step in zip(slices, (1, 3, 2)):
        copy.wait_recv()
        came = lax.rem(chip + CHIPS - step, CHIPS) * 2 + core
        there = pl.ds(pl.multiple_of(came * 128, 128), 128)
        onward = remote(weight.at[:, there], weight.at[:, there], pass_send.at[step], pass_recv.at[step], partner)
        onward.start()
        passes.append(onward)
    for onward in passes:
        onward.wait_recv()

    backward(of_view, view_res, view_probs)

    def return_view(step):
        peer = view_peer(step)
        remote(
            view_res.at[:, pl.ds(peer * 2, 2)], view_back.at[:, pl.ds(view * 2, 2)], send_sem.at[5], recv_sem.at[5],
            {"view": peer},
        ).start()

    each(1, VIEWS, return_view)
    view_back[:, pl.ds(view * 2, 2)] = view_res[:, pl.ds(view * 2, 2)]

    others = FRAMES - 1
    remote(
        own.at[3, pl.ds(0, others)], of_frame.at[3, pl.ds(0, others)], send_sem.at[2], recv_sem.at[2], partner
    ).wait_recv()
    grad_rows(of_frame)
    frame_bias = group_bias(8)

    def rows_of_half(half, source, target, slot):
        lanes = pl.ds(half * HALF, HALF)
        parts = pl.ds(0, 3) if slot < 5 else pl.ds(0, 4)
        return remote(
            source.at[parts, pl.ds(0, others), :, lanes], target.at[parts, pl.ds(0, others), :, lanes],
            send_sem.at[slot], recv_sem.at[slot], partner,
        )

    def return_frame(half):
        lanes = pl.ds(half * HALF, HALF)

        def send(step):
            peer = frame_peer(step)
            remote(
                frame_res.at[:, peer, :, lanes], frame_back.at[:, frame, :, lanes],
                send_sem.at[6 + half], recv_sem.at[6 + half], {"frame": peer},
            ).start()

        return send

    def frame_step(pair):
        lanes = lanes_of(pair)
        query, key, value = (flat(of_frame[index, :, :, lanes]) for index in range(3))
        probs, out = forward_pair(query, key, value, frame_bias, lower)
        frame_res[0, :, :, lanes] = blocks(out.astype(BF16))
        backward_step(of_frame, frame_res, probs, pair)

    for half in range(2):
        rows_of_half(half, own, of_frame, 3 + half).wait_recv()

        def two(index):
            frame_step(half * (PAIRS // 2) + index * 2)
            frame_step(half * (PAIRS // 2) + index * 2 + 1)

        each(0, PAIRS // 4, two)
        each(1, FRAMES, return_frame(half))
        wide = slice(half * HALF, half * HALF + HALF)
        frame_back[:, pl.ds(frame, 1), :, wide] = frame_res[:, pl.ds(frame, 1), :, wide]

    for index, source in enumerate((own, of_view, of_frame)):
        rows[128 * index : 128 * index + 128] = flat(source[3])

    def gradient_rows(which):
        lanes = lanes_of(which)
        left = jnp.concatenate(
            [flat(res[0, :, :, lanes]) for res in (own_res, view_res, frame_res)], axis=0
        )
        return [dot(left, rows[:, HALF * part : HALF * part + HALF], TN) for part in range(2)]

    to_core = []
    for slot, step in enumerate((1, 3, 2, 0)):
        for part, value in enumerate(gradient_rows(chip_peer(step) * 2 + 1 - core)):
            core_out[slot, :, :, HALF * part : HALF * part + HALF] = blocks(value.astype(BF16))
        copy = remote(core_out.at[slot], core_in.at[slot], core_send.at[slot], core_recv.at[slot], partner)
        copy.start()
        to_core.append(copy)
    to_chip = []
    for slot, step in enumerate((1, 3, 2, 0)):
        values = gradient_rows(chip_peer(step) * 2 + core)
        to_core[slot].wait_recv()
        for part, value in enumerate(values):
            wide = slice(HALF * part, HALF * part + HALF)
            chip_out[slot, :, :, wide] = blocks((value + flat(core_in[slot, :, :, wide]).astype(F32)).astype(BF16))
        if step > 0:
            copy = remote(
                chip_out.at[slot], chip_in.at[slot], chip_send.at[slot], chip_recv.at[slot], chip_device(step)
            )
            copy.start()
            to_chip.append(copy)

    backward(own, own_res, own_probs)

    for copy in to_chip:
        copy.wait_recv()
    for part in range(4):
        wide = slice(256 * part, 256 * part + 256)
        total = chip_out[3, :, :, wide].astype(F32)
        for slot in range(3):
            total = total + chip_in[slot, :, :, wide].astype(F32)
        frame_out[:, :, wide] = total.astype(BF16)

    def send_gradient(step):
        peer = frame_peer(step)
        remote(frame_out.at[peer], frame_in.at[frame], send_sem.at[8], recv_sem.at[8], {"frame": peer}).start()

    each(1, FRAMES, send_gradient)
    frame_in[pl.ds(frame, 1)] = frame_out[pl.ds(frame, 1)]

    remote(
        view_res.at[:, pl.ds(0, 2 * (VIEWS - 1))], view_back.at[:, pl.ds(0, 2 * (VIEWS - 1))], send_sem.at[5],
        recv_sem.at[5], partner,
    ).wait_recv()
    for half in range(2):
        rows_of_half(half, frame_res, frame_back, 6 + half).wait_recv()
        for index in range(4):
            for part in range(2):
                wide = slice(half * HALF + 256 * part, half * HALF + 256 * part + 256)
                total = own_res[index, :, :, wide].astype(F32) + view_back[index, :, :, wide].astype(F32)
                total = total + frame_back[index, :, :, wide].astype(F32)
                results[index, :, :, wide] = total.astype(BF16)
    stores = []
    for index, target in ((1, dq_hbm), (2, dk_hbm), (3, dv_hbm)):
        stores.append(pltpu.make_async_copy(results.at[index], target, store_sem.at[index]))
    for store in stores:
        store.start()
    attended = flat(results[0])
    for part in range(4):
        wide = slice(256 * part, 256 * part + 256)
        own_res[0, :, :, wide] = blocks(dot(attended, weight[:, wide], NN).astype(BF16))
    stores.append(pltpu.make_async_copy(own_res.at[0], proj_hbm, store_sem.at[0]))
    stores[-1].start()

    remote(
        frame_out.at[pl.ds(0, others)], frame_in.at[pl.ds(0, others)], send_sem.at[8], recv_sem.at[8], partner
    ).wait_recv()
    total = frame_in[0].astype(F32)
    for index in range(1, FRAMES):
        total = total + frame_in[index].astype(F32)
    sample_out[...] = total
    to_sample = []
    for step in (1, 2, 3):
        copy = remote(
            sample_out, sample_in.at[step], core_send.at[3 + step], core_recv.at[3 + step], {"dp": sample_peer(step)}
        )
        copy.start()
        to_sample.append(copy)
    for copy in to_sample:
        copy.wait_recv()
    total = sample_out[...]
    for step in (1, 2, 3):
        total = total + sample_in[step]
    last[...] = (total * (1.0 / 256.0)).astype(BF16)
    stores.append(pltpu.make_async_copy(last, wg_hbm, store_sem.at[4]))
    stores[-1].start()

    weight_bytes = weight.at[pl.ds(0, 64 * (FRAMES - 1)), columns]
    remote(weight_bytes, weight_bytes, send_sem.at[0], recv_sem.at[0], partner).wait_send()
    view_bytes.wait_send()
    remote(
        own.at[3, pl.ds(0, others)], of_frame.at[3, pl.ds(0, others)], send_sem.at[2], recv_sem.at[2], partner
    ).wait_send()
    for half in range(2):
        rows_of_half(half, own, of_frame, 3 + half).wait_send()
        rows_of_half(half, frame_res, frame_back, 6 + half).wait_send()
    remote(
        view_res.at[:, pl.ds(0, 2 * (VIEWS - 1))], view_back.at[:, pl.ds(0, 2 * (VIEWS - 1))], send_sem.at[5],
        recv_sem.at[5], partner,
    ).wait_send()
    remote(
        frame_out.at[pl.ds(0, others)], frame_in.at[pl.ds(0, others)], send_sem.at[8], recv_sem.at[8], partner
    ).wait_send()
    for copy in slices + passes + to_core + to_chip + to_sample:
        copy.wait_send()
    for store in stores:
        store.wait()


def local(query_rows, key_rows, value_rows, cotangent, out_weight):
    shape = query_rows.shape
    tokens = (16, 8, D)
    rows = [array.reshape(tokens) for array in (query_rows, key_rows, value_rows, cotangent)]
    four = pltpu.VMEM((4,) + tokens, BF16)
    probs = pltpu.VMEM((PAIRS, 256, 128), F32)
    dma = pltpu.SemaphoreType.DMA
    out = jax.ShapeDtypeStruct(tokens, BF16)
    outs = pl.pallas_call(
        kernel,
        out_shape=(out, out, out, out, jax.ShapeDtypeStruct((8, D), BF16)),
        in_specs=[pl.BlockSpec(memory_space=pl.ANY)] * 5,
        out_specs=(pl.BlockSpec(memory_space=pl.ANY),) * 5,
        scratch_shapes=[
            four, four, four, pltpu.VMEM((64, D), BF16), pltpu.VMEM((D, D), BF16),
            four, four, four, four, four,
            probs, probs, pltpu.VMEM((128, D), BF16), pltpu.VMEM((384, D), BF16),
            four, four, four, four, pltpu.VMEM(tokens, BF16), pltpu.VMEM(tokens, BF16),
            pltpu.VMEM((8, D), F32), pltpu.VMEM((4, 8, D), F32),
            four, pltpu.VMEM((8, D), BF16),
            dma((5,)), dma((5,)), dma((9,)), dma((9,)), dma((8,)), dma((8,)), dma((4,)), dma((4,)),
            dma((4,)), dma((4,)), dma((4,)), dma((4,)),
        ],
        compiler_params=pltpu.CompilerParams(
            collective_id=0, has_side_effects=True, vmem_limit_bytes=52 * 2**20
        ),
        name="attention",
    )(*rows, out_weight)
    return tuple(array.reshape(shape) for array in outs[:4]) + (outs[4],)


def solution(mesh):
    tokens = P("dp", "view", "frame", None, None)
    return jax.shard_map(
        local,
        mesh=mesh,
        in_specs=(tokens, tokens, tokens, tokens, P("frame", None)),
        out_specs=(tokens, tokens, tokens, tokens, P(("view", "frame"), None)),
        check_vma=False,
    )
```

time: 1010 us -> 100 us (0.10)
  the two profiles are of different devices: /device:TPU:64 before, /device:TPU:1 now
where the time goes in v1:
time: 100 us; the launch traced here: 99.4 us
  Pallas kernels  91.6 us (92%)
  local copies, waits for them, and re-layouts  7.16 us (7%)
    pallas_call x1, Pallas kernels, local(): pl.pallas_call(kernel, out_shape=(out, out, out, out, jax.ShapeDtypeStruc...  91.6 us
    unnamed x13, local copies, waits for them, and re-layouts  7.16 us

profile of v1, /device:TPU:1, one launch (start us, length us, event | category | flops | bytes accessed | tf_op | source)
XLA Modules:
  0.0 99.4 jit_solution(1878700028619806973)
XLA Ops:
  0.6 0.0 copy-start
  0.6 0.9 copy-done
  1.6 0.0 copy-start.1
  1.6 0.9 copy-done.1
  2.5 0.0 copy-start.2
  2.5 0.9 copy-done.2
  3.5 0.0 copy-start.3
  3.5 0.9 copy-done.3
  4.4 91.6 %attention.1 = (bf16[16,8,1024]{2,1,0:T(8,128)(2,1)S(1)}, bf16[16,8,1024]{2,1,0:T(8,128)(2,1)S(1)}, bf16[16,8,1024]{2,1,0:T(8,128)(2,1)S(1)}, bf16[16,8,1024]{2,1,0:T(8,128)(2,1)S(1)}, bf16[8,1024]{1,0:T(8,128)(2,1)S(1)}) custom-call(bf16[16,8,1024]{2,1,0:T(8,128)(2,1)S(1)} %bitcast.12, bf16[16,8,1024]{2,1,0:T(8,128)(2,1)S(1)} %bitcast.13, ...), custom_call_target="tpu_custom_call" | custom-call | tf_op jit(solution)/shard_map/attention/pallas_call | solution.py:465
  96.0 0.7 copy.15
  96.7 0.7 copy.16
  97.4 0.7 copy.17
  98.1 0.7 copy.18
  98.8 0.6 copy.19
Async XLA Ops:
  0.6 1.0 copy-start
  1.6 0.9 copy-start.1
  2.5 0.9 copy-start.2
  3.5 0.9 copy-start.3

commit v2 on v1

v2 whole, which is shorter than its diff:
```python
import functools

import jax
import jax.numpy as jnp
from jax import lax
from jax.experimental import pallas as pl
from jax.experimental.pallas import tpu as pltpu
from jax.sharding import PartitionSpec as P

F32 = jnp.float32
BF16 = jnp.bfloat16
MESH = pl.DeviceIdType.MESH
NN = (((1,), (0,)), ((), ()))
NT = (((1,), (1,)), ((), ()))
TN = (((0,), (0,)), ((), ()))
MASKED = -1e30

D = 1024
VIEWS = 8
FRAMES = 16
CHIPS = VIEWS // 2
PAIRS = D // 128
HALF = D // 2
SCALE = 0.125


def dot(left, right, dims):
    return lax.dot_general(left, right, dims, preferred_element_type=F32)


def flat(block):
    return block.reshape(block.shape[0] * block.shape[1], block.shape[2])


def blocks(rows):
    return rows.reshape(rows.shape[0] // 8, 8, rows.shape[1])


def lower_lanes():
    return lax.broadcasted_iota(jnp.int32, (128, 128), 1) < 64


def by_head(rows, lower):
    one = lower.astype(F32).astype(BF16)
    other = (1.0 - lower.astype(F32)).astype(BF16)
    return jnp.concatenate([rows * one, rows * other], axis=0)


def group_bias(modulus):
    row = lax.broadcasted_iota(jnp.int32, (128, 128), 0)
    column = lax.broadcasted_iota(jnp.int32, (128, 128), 1)
    same = lax.rem(row, modulus) == lax.rem(column, modulus)
    return jnp.where(same, 0.0, MASKED).astype(F32)


def forward_pair(query, key, value, bias, lower):
    scores = dot(by_head(key, lower), query, NT) * SCALE
    halves = []
    for head in range(2):
        part = scores[128 * head : 128 * head + 128]
        if bias is not None:
            part = part + bias
        raised = jnp.exp(part - jnp.max(part, axis=0, keepdims=True))
        halves.append(raised * (1.0 / jnp.sum(raised, axis=0, keepdims=True)))
    probs = jnp.concatenate(halves, axis=0)
    out = dot(probs.astype(BF16), by_head(value, lower), TN)
    return probs, out


def backward_pair(query, key, value, grad, probs, lower):
    dprob = dot(by_head(value, lower), grad, NT)
    halves = []
    for head in range(2):
        prob = probs[128 * head : 128 * head + 128]
        term = prob * dprob[128 * head : 128 * head + 128]
        halves.append((term - prob * jnp.sum(term, axis=0, keepdims=True)).astype(BF16))
    dscore = jnp.concatenate(halves, axis=0)
    value_grad = dot(probs.astype(BF16), grad, NN)
    value_grad = jnp.where(lower, value_grad[:128], value_grad[128:])
    key_grad = dot(dscore, query, NN)
    key_grad = jnp.where(lower, key_grad[:128], key_grad[128:]) * SCALE
    query_grad = dot(dscore, by_head(key, lower), TN) * SCALE
    return query_grad, key_grad, value_grad


def frame_offset(step):
    far = lax.rem(step, 2)
    turn = step // 2
    odd = lax.rem(turn, 2)
    near = odd * ((turn + 1) // 2) + (1 - odd) * lax.rem(8 - turn // 2, 8)
    return near, far


def kernel(
    q_hbm, k_hbm, v_hbm, c_hbm, w_hbm,
    proj_hbm, dq_hbm, dk_hbm, dv_hbm, wg_hbm,
    own, of_view, of_frame, shard, weight,
    own_res, view_res, frame_res, view_back, frame_back,
    own_probs, view_probs, frame_probs, grad, frame_grad, rows,
    core_out, core_in, chip_out, chip_in, near_out, near_in, far_out, far_in,
    results, last,
    load_sem, store_sem, send_sem, recv_sem, core_send, core_recv, chip_send, chip_recv,
    slice_send, slice_recv, pass_send, pass_recv,
):
    sample = lax.axis_index("dp")
    view = lax.axis_index("view")
    frame = lax.axis_index("frame")
    chip = view // 2
    core = lax.rem(view, 2)
    far = frame // 8
    near = lax.rem(frame, 8)
    column = far * 4 + sample
    partner = {"view": chip * 2 + 1 - core}
    opposite = lax.rem(far + 1, 2) * 8 + near
    low = lax.rem(chip, 2)
    halves = (1 - chip // 2, chip // 2)
    others = FRAMES - 1

    def frame_peer(step):
        by, across = frame_offset(step)
        return lax.rem(far + across, 2) * 8 + lax.rem(near + by, 8)

    def near_peer(step):
        by, _ = frame_offset(step * 2)
        return lax.rem(near + by, 8)

    def view_peer(step):
        return lax.rem(view + step, VIEWS)

    def column_device(step):
        other = lax.rem(column + step, 8)
        return {"dp": lax.rem(other, 4), "frame": (other // 4) * 8 + near}, other

    def chip_peer(step):
        return lax.rem(chip + step, CHIPS)

    def chip_device(step):
        return {"view": chip_peer(step) * 2 + core}

    def remote(source, target, send, recv, device):
        return pltpu.make_async_remote_copy(
            src_ref=source, dst_ref=target, send_sem=send, recv_sem=recv,
            device_id=device, device_id_type=MESH,
        )

    def group(source, target, slot):
        return remote(source, target, send_sem.at[slot], recv_sem.at[slot], partner)

    def each(first, last_step, body):
        def step(index, carry):
            body(index)
            return carry

        lax.fori_loop(first, last_step, step, 0)

    with jax.named_scope("load_and_greet"):
        loads = [pltpu.make_async_copy(w_hbm, shard, load_sem.at[4])]
        for index, source in enumerate((q_hbm, k_hbm, v_hbm, c_hbm)):
            loads.append(pltpu.make_async_copy(source, own.at[index], load_sem.at[index]))
        for load in loads:
            load.start()
        barrier = pltpu.get_barrier_semaphore()

        def greet(device):
            pl.semaphore_signal(barrier, inc=1, device_id=device, device_id_type=MESH)

        each(1, FRAMES, lambda step: greet({"frame": frame_peer(step)}))
        each(1, VIEWS, lambda step: greet({"view": view_peer(step)}))
        each(1, 4, lambda step: greet(column_device(step)[0]))
        each(5, 8, lambda step: greet(column_device(step)[0]))
        pl.semaphore_wait(barrier, FRAMES - 1 + VIEWS - 1 + 6)
        for load in loads:
            load.wait()

    columns = pl.ds(pl.multiple_of(view * 128, 128), 128)

    def shard_rows(which):
        return pl.ds(pl.multiple_of(which * 64, 64), 64)

    across = remote(
        shard.at[:, columns], weight.at[shard_rows(frame), columns], slice_send.at[0], slice_recv.at[0],
        {"frame": opposite},
    )

    def send_weight(source, which, slot):
        def send(step):
            remote(
                source, weight.at[shard_rows(which), columns], send_sem.at[slot], recv_sem.at[slot],
                {"frame": far * 8 + near_peer(step)},
            ).start()

        return send

    def near_weight(slot):
        part = weight.at[pl.ds(0, 64 * 7), columns]
        return group(part, part, slot)

    def send_view(step):
        peer = view_peer(step)
        remote(
            own.at[:, pl.ds(peer * 2, 2)], of_view.at[:, pl.ds(view * 2, 2)], send_sem.at[1], recv_sem.at[1],
            {"view": peer},
        ).start()

    def view_group(source, target, first, count, slot):
        parts, most = pl.ds(first, count), pl.ds(0, 2 * (VIEWS - 1))
        return group(source.at[parts, most], target.at[parts, most], slot)

    def send_frame_grad(step):
        peer = frame_peer(step)
        remote(own.at[3, peer], of_frame.at[3, frame], send_sem.at[2], recv_sem.at[2], {"frame": peer}).start()

    def frame_group(source, target, first, count, lanes, slot):
        parts, most = pl.ds(first, count), pl.ds(0, others)
        return group(source.at[parts, most, :, lanes], target.at[parts, most, :, lanes], slot)

    def lanes_of_half(half):
        return pl.ds(pl.multiple_of(halves[half] * HALF, HALF), HALF)

    def send_frame_rows(half):
        lanes = lanes_of_half(half)

        def send(step):
            peer = frame_peer(step)
            remote(
                own.at[pl.ds(0, 3), peer, :, lanes], of_frame.at[pl.ds(0, 3), frame, :, lanes],
                send_sem.at[3 + half], recv_sem.at[3 + half], {"frame": peer},
            ).start()

        return send

    with jax.named_scope("send_first"):
        across.start()
        each(1, 8, send_weight(shard.at[:, columns], frame, 0))
        each(1, VIEWS, send_view)
        weight[shard_rows(frame), columns] = shard[:, columns]
        of_frame[:, pl.ds(frame, 1)] = own[:, pl.ds(frame, 1)]
        of_view[:, pl.ds(view * 2, 2)] = own[:, pl.ds(view * 2, 2)]

    lower = lower_lanes()

    def lanes_of(pair):
        return pl.ds(pl.multiple_of(pair * 128, 128), 128)

    def forward(source, target, kept, bias, first=0, count=PAIRS):
        def step(pair):
            lanes = lanes_of(pair)
            query, key, value = (flat(source[index, :, :, lanes]) for index in range(3))
            probs, out = forward_pair(query, key, value, bias, lower)
            kept[pair] = probs
            target[0, :, :, lanes] = blocks(out.astype(BF16))

        def two(index):
            step(first + index * 2)
            step(first + index * 2 + 1)

        each(0, count // 2, two)

    def grad_rows(source, target):
        cotangent = flat(source[3])
        for part in range(4):
            wide = slice(256 * part, 256 * part + 256)
            target[:, wide] = dot(cotangent, weight[wide, :], NT).astype(BF16)

    def backward(source, target, kept, grad, first=0, count=PAIRS):
        def step(pair):
            lanes = lanes_of(pair)
            query, key, value = (flat(source[index, :, :, lanes]) for index in range(3))
            grads = backward_pair(query, key, value, grad[:, lanes], kept[pair], lower)
            for index, term in enumerate(grads):
                target[1 + index, :, :, lanes] = blocks(term.astype(BF16))

        def two(index):
            step(first + index * 2)
            step(first + index * 2 + 1)

        each(0, count // 2, two)

    with jax.named_scope("spatial_forward"):
        forward(own, own_res, own_probs, None, 0, PAIRS // 2)
    with jax.named_scope("wait_weight_opposite"):
        across.wait_recv()
    with jax.named_scope("send_weight"):
        each(1, 8, send_weight(weight.at[shard_rows(opposite), columns], opposite, 10))
    with jax.named_scope("spatial_forward"):
        forward(own, own_res, own_probs, None, PAIRS // 2, PAIRS // 2)
    with jax.named_scope("send_frames"):
        each(1, FRAMES, send_frame_rows(0))
        each(1, FRAMES, send_frame_grad)
        each(1, FRAMES, send_frame_rows(1))

    with jax.named_scope("wait_weight_frames"):
        near_weight(0).wait_recv()
        near_weight(10).wait_recv()
    def slice_of(step, first, count):
        came = chip_peer(CHIPS - step) * 2 + core
        return weight.at[pl.ds(first, count), pl.ds(pl.multiple_of(came * 128, 128), 128)]

    def along(step, first, count, index, to):
        part = slice_of(step, first, count)
        copy = remote(part, part, slice_send.at[index], slice_recv.at[index], chip_device(to))
        copy.start()
        return copy

    def to_partner(step, first, count, index):
        part = slice_of(step, first, count)
        copy = remote(part, part, pass_send.at[index], pass_recv.at[index], partner)
        copy.start()
        return copy

    with jax.named_scope("pass_weight"):
        slices = [along(0, 0, D, 1, 1), along(0, 0, D, 3, 3)]
        passes = [to_partner(0, 0, D, 0)]

    with jax.named_scope("wait_view_rows"):
        view_group(own, of_view, 0, 4, 1).wait_recv()
    with jax.named_scope("view_forward"):
        forward(of_view, view_res, view_probs, group_bias(16))

    with jax.named_scope("wait_weight_chips"):
        slices[0].wait_recv()
        slices.append(along(1, 0, HALF, 2, 1))
        slices[1].wait_recv()
        slices.append(along(3, HALF, HALF, 4, 3))
        passes.append(to_partner(1, 0, D, 1))
        passes.append(to_partner(3, 0, D, 3))
    def return_view():
        def send(step):
            peer = view_peer(step)
            remote(
                view_res.at[:, pl.ds(peer * 2, 2)], view_back.at[:, pl.ds(view * 2, 2)],
                send_sem.at[5], recv_sem.at[5], {"view": peer},
            ).start()

        each(1, VIEWS, send)
        view_back[:, pl.ds(view * 2, 2)] = view_res[:, pl.ds(view * 2, 2)]

    def return_frame(half, first, count, slot):
        lanes = lanes_of_half(half)
        parts = pl.ds(first, count)

        def send(step):
            peer = frame_peer(step)
            remote(
                frame_res.at[parts, peer, :, lanes], frame_back.at[parts, frame, :, lanes],
                send_sem.at[slot], recv_sem.at[slot], {"frame": peer},
            ).start()

        each(1, FRAMES, send)
        for index in range(first, first + count):
            frame_back[index, pl.ds(frame, 1), :, lanes] = frame_res[index, pl.ds(frame, 1), :, lanes]

    everything = pl.ds(0, D)
    frame_bias = group_bias(8)

    def frame_forward(half):
        with jax.named_scope("wait_frame_rows"):
            frame_group(own, of_frame, 0, 3, lanes_of_half(half), 3 + half).wait_recv()
        with jax.named_scope("frame_forward"):
            forward(of_frame, frame_res, frame_probs, frame_bias, halves[half] * (PAIRS // 2), PAIRS // 2)

    def frame_backward(half):
        with jax.named_scope("frame_backward"):
            backward(of_frame, frame_res, frame_probs, frame_grad, halves[half] * (PAIRS // 2), PAIRS // 2)

    targets = (halves[0] * 2 + low, halves[0] * 2 + 1 - low, halves[1] * 2 + 1 - low, chip)

    def gradient_rows(which):
        lanes = lanes_of(which)
        left = jnp.concatenate(
            [flat(res[0, :, :, lanes]) for res in (own_res, view_res, frame_res)], axis=0
        )
        return [dot(left, rows[:, HALF * part : HALF * part + HALF], TN) for part in range(2)]

    to_core, to_chip = [], []

    def gradient_to_chips(half):
        with jax.named_scope("gradient_to_core"):
            for slot in (2 * half, 2 * half + 1):
                for part, value in enumerate(gradient_rows(targets[slot] * 2 + 1 - core)):
                    core_out[slot, :, :, HALF * part : HALF * part + HALF] = blocks(value.astype(BF16))
                copy = remote(core_out.at[slot], core_in.at[slot], core_send.at[slot], core_recv.at[slot], partner)
                copy.start()
                to_core.append(copy)
        with jax.named_scope("gradient_to_chips"):
            for slot in (2 * half, 2 * half + 1):
                values = gradient_rows(targets[slot] * 2 + core)
                to_core[slot].wait_recv()
                for part, value in enumerate(values):
                    wide = slice(HALF * part, HALF * part + HALF)
                    total = value + flat(core_in[slot, :, :, wide]).astype(F32)
                    chip_out[slot, :, :, wide] = blocks(total.astype(BF16))
                if slot < 3:
                    copy = remote(
                        chip_out.at[slot], chip_in.at[slot], chip_send.at[slot], chip_recv.at[slot],
                        {"view": targets[slot] * 2 + core},
                    )
                    copy.start()
                    to_chip.append(copy)

    frame_forward(0)
    with jax.named_scope("wait_weight_chips"):
        slices[2].wait_recv()
        passes.append(to_partner(2, 0, HALF, 2))
        slices[3].wait_recv()
        passes.append(to_partner(2, HALF, HALF, 4))

    with jax.named_scope("wait_frame_cotangent"):
        frame_group(own, of_frame, 3, 1, everything, 2).wait_recv()
    for index, source in enumerate((own, of_view, of_frame)):
        rows[128 * index : 128 * index + 128] = flat(source[3])
    gradient_to_chips(0)
    with jax.named_scope("wait_weight_core"):
        for onward in passes:
            onward.wait_recv()
    with jax.named_scope("frame_grad"):
        grad_rows(of_frame, frame_grad)
    frame_backward(0)
    with jax.named_scope("return_frame"):
        return_frame(0, 0, 4, 6)

    frame_forward(1)
    gradient_to_chips(1)
    frame_backward(1)
    with jax.named_scope("return_frame"):
        return_frame(1, 0, 2, 7)

    with jax.named_scope("view_backward"):
        grad_rows(of_view, grad)
        backward(of_view, view_res, view_probs, grad)
    with jax.named_scope("return_view"):
        return_view()

    def gradient_near():
        most = pl.ds(0, 7)
        return group(near_out.at[:, most], near_in.at[:, most], 8)

    def gradient_far():
        part = far_in.at[pl.ds(0, 7)]
        return group(part, part, 9)

    def send_near(step):
        peer = near_peer(step)
        remote(
            near_out.at[:, peer], near_in.at[:, near], send_sem.at[8], recv_sem.at[8], {"frame": far * 8 + peer}
        ).start()

    def send_far(step):
        device, other = column_device(step)
        remote(far_out.at[other // 4], far_in.at[column], send_sem.at[9], recv_sem.at[9], device).start()

    with jax.named_scope("wait_gradient_chips"):
        for copy in to_chip:
            copy.wait_recv()
    with jax.named_scope("gradient_to_near"):
        for part in range(4):
            wide = slice(256 * part, 256 * part + 256)
            total = chip_out[3, :, :, wide].astype(F32)
            for slot in range(3):
                total = total + chip_in[slot, :, :, wide].astype(F32)
            for index in range(2):
                near_out[index, :, :, wide] = total[8 * index : 8 * index + 8].astype(BF16)
        each(1, 8, send_near)
        near_in[:, pl.ds(near, 1)] = near_out[:, pl.ds(near, 1)]

    with jax.named_scope("spatial_backward"):
        grad_rows(own, grad)
        backward(own, own_res, own_probs, grad)
    with jax.named_scope("return_frame"):
        return_frame(1, 2, 2, 11)

    with jax.named_scope("wait_gradient_near"):
        gradient_near().wait_recv()
    with jax.named_scope("gradient_to_far"):
        for index in range(2):
            total = near_in[index, 0].astype(F32)
            for peer in range(1, 8):
                total = total + near_in[index, peer].astype(F32)
            far_out[index] = total.astype(BF16)
        each(1, 8, send_far)
        far_in[pl.ds(column, 1)] = far_out[pl.ds(far, 1)]

    def add_terms(index, lanes):
        total = own_res[index, :, :, lanes].astype(F32) + view_back[index, :, :, lanes].astype(F32)
        total = total + frame_back[index, :, :, lanes].astype(F32)
        results[index, :, :, lanes] = total.astype(BF16)

    stores = []

    def put(source, target, slot):
        stores.append(pltpu.make_async_copy(source, target, store_sem.at[slot]))
        stores[-1].start()

    def columns_of(half, part):
        return pl.ds(pl.multiple_of(halves[half] * HALF + 256 * part, 256), 256)

    with jax.named_scope("wait_view_back"):
        view_group(view_res, view_back, 0, 4, 5).wait_recv()
    with jax.named_scope("wait_frame_back"):
        frame_group(frame_res, frame_back, 0, 4, lanes_of_half(0), 6).wait_recv()
    with jax.named_scope("add_terms"):
        for index in range(4):
            for part in range(2):
                add_terms(index, columns_of(0, part))

    with jax.named_scope("wait_frame_back"):
        frame_group(frame_res, frame_back, 0, 2, lanes_of_half(1), 7).wait_recv()
    with jax.named_scope("add_terms"):
        for index in range(2):
            for part in range(2):
                add_terms(index, columns_of(1, part))
    put(results.at[1], dq_hbm, 1)
    with jax.named_scope("project"):
        attended = flat(results[0])
        for part in range(4):
            wide = slice(256 * part, 256 * part + 256)
            own_res[0, :, :, wide] = blocks(dot(attended, weight[:, wide], NN).astype(BF16))
        put(own_res.at[0], proj_hbm, 0)

    with jax.named_scope("wait_frame_back"):
        frame_group(frame_res, frame_back, 2, 2, lanes_of_half(1), 11).wait_recv()
    with jax.named_scope("add_terms"):
        for index in range(2, 4):
            for part in range(2):
                add_terms(index, columns_of(1, part))
    put(results.at[2], dk_hbm, 2)
    put(results.at[3], dv_hbm, 3)

    with jax.named_scope("wait_gradient_far"):
        gradient_far().wait_recv()
    total = far_in[0].astype(F32)
    for index in range(1, 8):
        total = total + far_in[index].astype(F32)
    last[...] = (total * (1.0 / 256.0)).astype(BF16)
    put(last, wg_hbm, 4)

    with jax.named_scope("drain"):
        near_weight(0).wait_send()
        near_weight(10).wait_send()
        across.wait_send()
        view_group(own, of_view, 0, 4, 1).wait_send()
        view_group(view_res, view_back, 0, 4, 5).wait_send()
        frame_group(own, of_frame, 3, 1, everything, 2).wait_send()
        for half in range(2):
            frame_group(own, of_frame, 0, 3, lanes_of_half(half), 3 + half).wait_send()
        frame_group(frame_res, frame_back, 0, 4, lanes_of_half(0), 6).wait_send()
        frame_group(frame_res, frame_back, 0, 2, lanes_of_half(1), 7).wait_send()
        frame_group(frame_res, frame_back, 2, 2, lanes_of_half(1), 11).wait_send()
        gradient_far().wait_send()
        gradient_near().wait_send()
        for copy in slices + passes + to_core + to_chip:
            copy.wait_send()
        for copy in stores:
            copy.wait()


def store(*refs):
    copies = [pltpu.make_async_copy(refs[index], refs[5 + index], refs[10].at[index]) for index in range(5)]
    for copy in copies:
        copy.start()
    for copy in copies:
        copy.wait()


def local(query_rows, key_rows, value_rows, cotangent, out_weight):
    shape = query_rows.shape
    tokens = (16, 8, D)
    rows = [array.reshape(tokens) for array in (query_rows, key_rows, value_rows, cotangent)]
    rows = [pltpu.with_memory_space_constraint(array, pltpu.HBM) for array in rows + [out_weight]]
    four = pltpu.VMEM((4,) + tokens, BF16)
    near = pltpu.VMEM((2, 8, 8, D), BF16)
    probs = pltpu.VMEM((PAIRS, 256, 128), F32)
    dma = pltpu.SemaphoreType.DMA
    out = jax.ShapeDtypeStruct(tokens, BF16)
    outs = pl.pallas_call(
        kernel,
        out_shape=(out, out, out, out, jax.ShapeDtypeStruct((8, D), BF16)),
        in_specs=[pl.BlockSpec(memory_space=pltpu.HBM)] * 5,
        out_specs=(pl.BlockSpec(memory_space=pl.ANY),) * 5,
        scratch_shapes=[
            four, four, four, pltpu.VMEM((64, D), BF16), pltpu.VMEM((D, D), BF16),
            four, four, four, four, four,
            probs, probs, probs, pltpu.VMEM((128, D), BF16), pltpu.VMEM((128, D), BF16), pltpu.VMEM((384, D), BF16),
            four, four, four, four, near, near, pltpu.VMEM((2, 8, D), BF16), pltpu.VMEM((8, 8, D), BF16),
            four, pltpu.VMEM((8, D), BF16),
            dma((5,)), dma((5,)), dma((13,)), dma((13,)), dma((4,)), dma((4,)), dma((4,)), dma((4,)),
            dma((5,)), dma((5,)), dma((5,)), dma((5,)),
        ],
        compiler_params=pltpu.CompilerParams(
            collective_id=0, has_side_effects=True, vmem_limit_bytes=52 * 2**20
        ),
        name="attention",
    )(*rows)
    outs = pl.pallas_call(
        store,
        out_shape=tuple(jax.ShapeDtypeStruct(array.shape, BF16) for array in outs),
        in_specs=[pl.BlockSpec(memory_space=pl.ANY)] * 5,
        out_specs=(pl.BlockSpec(memory_space=pltpu.HBM),) * 5,
        scratch_shapes=[dma((5,))],
        compiler_params=pltpu.CompilerParams(vmem_limit_bytes=2**20),
        name="store",
    )(*outs)
    return tuple(array.reshape(shape) for array in outs[:4]) + (outs[4],)


def solution(mesh):
    tokens = P("dp", "view", "frame", None, None)
    return jax.shard_map(
        local,
        mesh=mesh,
        in_specs=(tokens, tokens, tokens, tokens, P("frame", None)),
        out_specs=(tokens, tokens, tokens, tokens, P(("view", "frame"), None)),
        check_vma=False,
    )
```

time: 100 us -> 85.4 us (0.85)
  local copies, waits for them, and re-layouts: 7.16 us -> 0 us
  Pallas kernels: 91.6 us -> 84.6 us
    pallas_call x1, Pallas kernels: 91.6 us -> 83.6 us  [local(): pl.pallas_call(kernel, out_shape=(out, out, out, out, jax.ShapeDtypeStruc...]
    unnamed x13 -> x0, local copies, waits for them, and re-layouts: 7.16 us -> none
    pallas_call x0 -> x1, Pallas kernels: none -> 1.01 us  [local(): pl.pallas_call(store, out_shape=tuple((jax.ShapeDtypeStruct(array.shape,...]
where the time goes in v2:
time: 85.4 us; the launch traced here: 85.3 us
  Pallas kernels  84.6 us (99%)
    pallas_call x1, Pallas kernels, local(): pl.pallas_call(kernel, out_shape=(out, out, out, out, jax.ShapeDtypeStruc...  83.6 us

profile of v2, /device:TPU:1, one launch (start us, length us, event | category | flops | bytes accessed | tf_op | source)
XLA Modules:
  0.0 85.3 jit_solution(1197221921014881201)
XLA Ops:
  0.6 83.6 %attention.1 = (bf16[16,8,1024]{2,1,0:T(8,128)(2,1)S(1)}, bf16[16,8,1024]{2,1,0:T(8,128)(2,1)S(1)}, bf16[16,8,1024]{2,1,0:T(8,128)(2,1)S(1)}, bf16[16,8,1024]{2,1,0:T(8,128)(2,1)S(1)}, bf16[8,1024]{1,0:T(8,128)(2,1)S(1)}) custom-call(bf16[16,8,1024]{2,1,0:T(8,128)(2,1)} %bitcast.8, bf16[16,8,1024]{2,1,0:T(8,128)(2,1)} %bitcast.9, ...), custom_call_target="tpu_custom_call" | custom-call | tf_op jit(solution)/shard_map/attention/pallas_call | solution.py:575
  84.2 1.0 %store.1 = (bf16[16,8,1024]{2,1,0:T(8,128)(2,1)}, bf16[16,8,1024]{2,1,0:T(8,128)(2,1)}, bf16[16,8,1024]{2,1,0:T(8,128)(2,1)}, bf16[16,8,1024]{2,1,0:T(8,128)(2,1)}, bf16[8,1024]{1,0:T(8,128)(2,1)}) custom-call(bf16[16,8,1024]{2,1,0:T(8,128)(2,1)S(1)} %get-tuple-element.15.refs_0_, bf16[16,8,1024]{2,1,0:T(8,128)(2,1)S(1)} %get-tuple-element.16.refs_1_, ...), custom_call_target="tpu_custom_call" | custom-call | tf_op jit(solution)/shard_map/store/pallas_call | solution.py:594

commit v3 on v2

--- a/solution.py
+++ b/solution.py
@@ -232,6 +232,7 @@
     with jax.named_scope("send_first"):
         across.start()
         each(1, 8, send_weight(shard.at[:, columns], frame, 0))
+        each(1, FRAMES, send_frame_grad)
         each(1, VIEWS, send_view)
         weight[shard_rows(frame), columns] = shard[:, columns]
         of_frame[:, pl.ds(frame, 1)] = own[:, pl.ds(frame, 1)]
@@ -286,8 +287,6 @@
         forward(own, own_res, own_probs, None, PAIRS // 2, PAIRS // 2)
     with jax.named_scope("send_frames"):
         each(1, FRAMES, send_frame_rows(0))
-        each(1, FRAMES, send_frame_grad)
-        each(1, FRAMES, send_frame_rows(1))
 
     with jax.named_scope("wait_weight_frames"):
         near_weight(0).wait_recv()
@@ -316,6 +315,8 @@
         view_group(own, of_view, 0, 4, 1).wait_recv()
     with jax.named_scope("view_forward"):
         forward(of_view, view_res, view_probs, group_bias(16))
+    with jax.named_scope("send_frames"):
+        each(1, FRAMES, send_frame_rows(1))
 
     with jax.named_scope("wait_weight_chips"):
         slices[0].wait_recv()
@@ -398,18 +399,17 @@
                     copy.start()
                     to_chip.append(copy)
 
-    frame_forward(0)
     with jax.named_scope("wait_weight_chips"):
         slices[2].wait_recv()
         passes.append(to_partner(2, 0, HALF, 2))
         slices[3].wait_recv()
         passes.append(to_partner(2, HALF, HALF, 4))
 
+    frame_forward(0)
+    with jax.named_scope("return_frame_out"):
+        return_frame(0, 0, 1, 6)
     with jax.named_scope("wait_frame_cotangent"):
         frame_group(own, of_frame, 3, 1, everything, 2).wait_recv()
-    for index, source in enumerate((own, of_view, of_frame)):
-        rows[128 * index : 128 * index + 128] = flat(source[3])
-    gradient_to_chips(0)
     with jax.named_scope("wait_weight_core"):
         for onward in passes:
             onward.wait_recv()
@@ -417,13 +417,18 @@
         grad_rows(of_frame, frame_grad)
     frame_backward(0)
     with jax.named_scope("return_frame"):
-        return_frame(0, 0, 4, 6)
+        return_frame(0, 1, 3, 13)
+    for index, source in enumerate((own, of_view, of_frame)):
+        rows[128 * index : 128 * index + 128] = flat(source[3])
+    gradient_to_chips(0)
 
     frame_forward(1)
+    with jax.named_scope("return_frame_out"):
+        return_frame(1, 0, 1, 7)
     gradient_to_chips(1)
     frame_backward(1)
     with jax.named_scope("return_frame"):
-        return_frame(1, 0, 2, 7)
+        return_frame(1, 1, 1, 14)
 
     with jax.named_scope("view_backward"):
         grad_rows(of_view, grad)
@@ -463,12 +468,12 @@
         each(1, 8, send_near)
         near_in[:, pl.ds(near, 1)] = near_out[:, pl.ds(near, 1)]
 
+    with jax.named_scope("return_frame"):
+        return_frame(1, 2, 2, 11)
+
     with jax.named_scope("spatial_backward"):
         grad_rows(own, grad)
         backward(own, own_res, own_probs, grad)
-    with jax.named_scope("return_frame"):
-        return_frame(1, 2, 2, 11)
-
     with jax.named_scope("wait_gradient_near"):
         gradient_near().wait_recv()
     with jax.named_scope("gradient_to_far"):
@@ -497,14 +502,16 @@
     with jax.named_scope("wait_view_back"):
         view_group(view_res, view_back, 0, 4, 5).wait_recv()
     with jax.named_scope("wait_frame_back"):
-        frame_group(frame_res, frame_back, 0, 4, lanes_of_half(0), 6).wait_recv()
+        frame_group(frame_res, frame_back, 0, 1, lanes_of_half(0), 6).wait_recv()
+        frame_group(frame_res, frame_back, 1, 3, lanes_of_half(0), 13).wait_recv()
     with jax.named_scope("add_terms"):
         for index in range(4):
             for part in range(2):
                 add_terms(index, columns_of(0, part))
 
     with jax.named_scope("wait_frame_back"):
-        frame_group(frame_res, frame_back, 0, 2, lanes_of_half(1), 7).wait_recv()
+        frame_group(frame_res, frame_back, 0, 1, lanes_of_half(1), 7).wait_recv()
+        frame_group(frame_res, frame_back, 1, 1, lanes_of_half(1), 14).wait_recv()
     with jax.named_scope("add_terms"):
         for index in range(2):
             for part in range(2):
@@ -543,8 +550,10 @@
         frame_group(own, of_frame, 3, 1, everything, 2).wait_send()
         for half in range(2):
             frame_group(own, of_frame, 0, 3, lanes_of_half(half), 3 + half).wait_send()
-        frame_group(frame_res, frame_back, 0, 4, lanes_of_half(0), 6).wait_send()
-        frame_group(frame_res, frame_back, 0, 2, lanes_of_half(1), 7).wait_send()
+        frame_group(frame_res, frame_back, 0, 1, lanes_of_half(0), 6).wait_send()
+        frame_group(frame_res, frame_back, 1, 3, lanes_of_half(0), 13).wait_send()
+        frame_group(frame_res, frame_back, 0, 1, lanes_of_half(1), 7).wait_send()
+        frame_group(frame_res, frame_back, 1, 1, lanes_of_half(1), 14).wait_send()
         frame_group(frame_res, frame_back, 2, 2, lanes_of_half(1), 11).wait_send()
         gradient_far().wait_send()
         gradient_near().wait_send()
@@ -583,7 +592,7 @@
             probs, probs, probs, pltpu.VMEM((128, D), BF16), pltpu.VMEM((128, D), BF16), pltpu.VMEM((384, D), BF16),
             four, four, four, four, near, near, pltpu.VMEM((2, 8, D), BF16), pltpu.VMEM((8, 8, D), BF16),
             four, pltpu.VMEM((8, D), BF16),
-            dma((5,)), dma((5,)), dma((13,)), dma((13,)), dma((4,)), dma((4,)), dma((4,)), dma((4,)),
+            dma((5,)), dma((5,)), dma((15,)), dma((15,)), dma((4,)), dma((4,)), dma((4,)), dma((4,)),
             dma((5,)), dma((5,)), dma((5,)), dma((5,)),
         ],
         compiler_params=pltpu.CompilerParams(

time: 85.4 us -> 84 us (0.984)
  Pallas kernels: 84.6 us -> 82.5 us
    pallas_call x1, Pallas kernels: 83.6 us -> 81.5 us  [local(): pl.pallas_call(kernel, out_shape=(out, out, out, out, jax.ShapeDtypeStruc...]
where the time goes in v3:
time: 84 us; the launch traced here: 83.2 us
  Pallas kernels  82.5 us (98%)
    pallas_call x1, Pallas kernels, local(): pl.pallas_call(kernel, out_shape=(out, out, out, out, jax.ShapeDtypeStruc...  81.5 us

profile of v3, /device:TPU:1, one launch (start us, length us, event | category | flops | bytes accessed | tf_op | source)
XLA Modules:
  0.0 83.2 jit_solution(370862638804286409)
XLA Ops:
  0.6 81.5 %attention.1 = (bf16[16,8,1024]{2,1,0:T(8,128)(2,1)S(1)}, bf16[16,8,1024]{2,1,0:T(8,128)(2,1)S(1)}, bf16[16,8,1024]{2,1,0:T(8,128)(2,1)S(1)}, bf16[16,8,1024]{2,1,0:T(8,128)(2,1)S(1)}, bf16[8,1024]{1,0:T(8,128)(2,1)S(1)}) custom-call(bf16[16,8,1024]{2,1,0:T(8,128)(2,1)} %bitcast.8, bf16[16,8,1024]{2,1,0:T(8,128)(2,1)} %bitcast.9, ...), custom_call_target="tpu_custom_call" | custom-call | tf_op jit(solution)/shard_map/attention/pallas_call | solution.py:584
  82.2 1.0 %store.1 = (bf16[16,8,1024]{2,1,0:T(8,128)(2,1)}, bf16[16,8,1024]{2,1,0:T(8,128)(2,1)}, bf16[16,8,1024]{2,1,0:T(8,128)(2,1)}, bf16[16,8,1024]{2,1,0:T(8,128)(2,1)}, bf16[8,1024]{1,0:T(8,128)(2,1)}) custom-call(bf16[16,8,1024]{2,1,0:T(8,128)(2,1)S(1)} %get-tuple-element.15.refs_0_, bf16[16,8,1024]{2,1,0:T(8,128)(2,1)S(1)} %get-tuple-element.16.refs_1_, ...), custom_call_target="tpu_custom_call" | custom-call | tf_op jit(solution)/shard_map/store/pallas_call | solution.py:603

commit v4 on v3

--- a/solution.py
+++ b/solution.py
@@ -83,12 +83,17 @@
     return query_grad, key_grad, value_grad
 
 
+def near_offset(step):
+    turn = step - 1
+    odd = lax.rem(turn, 2)
+    return (turn // 2 + 1) * (1 - 2 * odd)
+
+
 def frame_offset(step):
-    far = lax.rem(step, 2)
-    turn = step // 2
+    across = lax.rem(step, 2)
+    turn = (step - 1) // 2
     odd = lax.rem(turn, 2)
-    near = odd * ((turn + 1) // 2) + (1 - odd) * lax.rem(8 - turn // 2, 8)
-    return near, far
+    return across * (4 + ((turn + 1) // 2) * (1 - 2 * odd)) + (1 - across) * near_offset(turn + 1), across
 
 
 def kernel(
@@ -115,14 +120,14 @@
     low = lax.rem(chip, 2)
     halves = (1 - chip // 2, chip // 2)
     others = FRAMES - 1
+    way = 1 - 2 * core
 
     def frame_peer(step):
         by, across = frame_offset(step)
-        return lax.rem(far + across, 2) * 8 + lax.rem(near + by, 8)
+        return lax.rem(far + across, 2) * 8 + lax.rem(near + way * by + 8, 8)
 
     def near_peer(step):
-        by, _ = frame_offset(step * 2)
-        return lax.rem(near + by, 8)
+        return lax.rem(near + way * near_offset(step) + 8, 8)
 
     def view_peer(step):
         return lax.rem(view + step, VIEWS)
@@ -164,10 +169,12 @@
         def greet(device):
             pl.semaphore_signal(barrier, inc=1, device_id=device, device_id_type=MESH)
 
-        each(1, FRAMES, lambda step: greet({"frame": frame_peer(step)}))
-        each(1, VIEWS, lambda step: greet({"view": view_peer(step)}))
-        each(1, 4, lambda step: greet(column_device(step)[0]))
-        each(5, 8, lambda step: greet(column_device(step)[0]))
+        for step in range(1, FRAMES):
+            greet({"frame": lax.rem(frame + step, FRAMES)})
+        for step in (1, 2, 3, 5, 6, 7):
+            greet(column_device(step)[0])
+        for step in range(1, VIEWS):
+            greet({"view": view_peer(step)})
         pl.semaphore_wait(barrier, FRAMES - 1 + VIEWS - 1 + 6)
         for load in loads:
             load.wait()
@@ -257,10 +264,10 @@
 
         each(0, count // 2, two)
 
-    def grad_rows(source, target):
+    def grad_rows(source, target, first=0, parts=4):
         cotangent = flat(source[3])
-        for part in range(4):
-            wide = slice(256 * part, 256 * part + 256)
+        for part in range(parts):
+            wide = pl.ds(pl.multiple_of(first + 256 * part, 256), 256)
             target[:, wide] = dot(cotangent, weight[wide, :], NT).astype(BF16)
 
     def backward(source, target, kept, grad, first=0, count=PAIRS):
@@ -361,6 +368,8 @@
             forward(of_frame, frame_res, frame_probs, frame_bias, halves[half] * (PAIRS // 2), PAIRS // 2)
 
     def frame_backward(half):
+        with jax.named_scope("frame_grad"):
+            grad_rows(of_frame, frame_grad, halves[half] * HALF, 2)
         with jax.named_scope("frame_backward"):
             backward(of_frame, frame_res, frame_probs, frame_grad, halves[half] * (PAIRS // 2), PAIRS // 2)
 
@@ -413,8 +422,6 @@
     with jax.named_scope("wait_weight_core"):
         for onward in passes:
             onward.wait_recv()
-    with jax.named_scope("frame_grad"):
-        grad_rows(of_frame, frame_grad)
     frame_backward(0)
     with jax.named_scope("return_frame"):
         return_frame(0, 1, 3, 13)
@@ -428,7 +435,7 @@
     gradient_to_chips(1)
     frame_backward(1)
     with jax.named_scope("return_frame"):
-        return_frame(1, 1, 1, 14)
+        return_frame(1, 1, 2, 14)
 
     with jax.named_scope("view_backward"):
         grad_rows(of_view, grad)
@@ -469,7 +476,7 @@
         near_in[:, pl.ds(near, 1)] = near_out[:, pl.ds(near, 1)]
 
     with jax.named_scope("return_frame"):
-        return_frame(1, 2, 2, 11)
+        return_frame(1, 3, 1, 11)
 
     with jax.named_scope("spatial_backward"):
         grad_rows(own, grad)
@@ -511,12 +518,13 @@
 
     with jax.named_scope("wait_frame_back"):
         frame_group(frame_res, frame_back, 0, 1, lanes_of_half(1), 7).wait_recv()
-        frame_group(frame_res, frame_back, 1, 1, lanes_of_half(1), 14).wait_recv()
+        frame_group(frame_res, frame_back, 1, 2, lanes_of_half(1), 14).wait_recv()
     with jax.named_scope("add_terms"):
-        for index in range(2):
+        for index in range(3):
             for part in range(2):
                 add_terms(index, columns_of(1, part))
     put(results.at[1], dq_hbm, 1)
+    put(results.at[2], dk_hbm, 2)
     with jax.named_scope("project"):
         attended = flat(results[0])
         for part in range(4):
@@ -525,12 +533,10 @@
         put(own_res.at[0], proj_hbm, 0)
 
     with jax.named_scope("wait_frame_back"):
-        frame_group(frame_res, frame_back, 2, 2, lanes_of_half(1), 11).wait_recv()
+        frame_group(frame_res, frame_back, 3, 1, lanes_of_half(1), 11).wait_recv()
     with jax.named_scope("add_terms"):
-        for index in range(2, 4):
-            for part in range(2):
-                add_terms(index, columns_of(1, part))
-    put(results.at[2], dk_hbm, 2)
+        for part in range(2):
+            add_terms(3, columns_of(1, part))
     put(results.at[3], dv_hbm, 3)
 
     with jax.named_scope("wait_gradient_far"):
@@ -553,8 +559,8 @@
         frame_group(frame_res, frame_back, 0, 1, lanes_of_half(0), 6).wait_send()
         frame_group(frame_res, frame_back, 1, 3, lanes_of_half(0), 13).wait_send()
         frame_group(frame_res, frame_back, 0, 1, lanes_of_half(1), 7).wait_send()
-        frame_group(frame_res, frame_back, 1, 1, lanes_of_half(1), 14).wait_send()
-        frame_group(frame_res, frame_back, 2, 2, lanes_of_half(1), 11).wait_send()
+        frame_group(frame_res, frame_back, 1, 2, lanes_of_half(1), 14).wait_send()
+        frame_group(frame_res, frame_back, 3, 1, lanes_of_half(1), 11).wait_send()
         gradient_far().wait_send()
         gradient_near().wait_send()
         for copy in slices + passes + to_core + to_chip:

time: 84 us -> 81.6 us (0.971)
  Pallas kernels: 82.5 us -> 80.3 us
    pallas_call x1, Pallas kernels: 81.5 us -> 79.3 us  [local(): pl.pallas_call(kernel, out_shape=(out, out, out, out, jax.ShapeDtypeStruc...]
where the time goes in v4:
time: 81.6 us; the launch traced here: 81 us
  Pallas kernels  80.3 us (98%)
    pallas_call x1, Pallas kernels, local(): pl.pallas_call(kernel, out_shape=(out, out, out, out, jax.ShapeDtypeStruc...  79.3 us

profile of v4, /device:TPU:1, one launch (start us, length us, event | category | flops | bytes accessed | tf_op | source)
XLA Modules:
  0.0 81.0 jit_solution(11930824121526465982)
XLA Ops:
  0.6 79.3 %attention.1 = (bf16[16,8,1024]{2,1,0:T(8,128)(2,1)S(1)}, bf16[16,8,1024]{2,1,0:T(8,128)(2,1)S(1)}, bf16[16,8,1024]{2,1,0:T(8,128)(2,1)S(1)}, bf16[16,8,1024]{2,1,0:T(8,128)(2,1)S(1)}, bf16[8,1024]{1,0:T(8,128)(2,1)S(1)}) custom-call(bf16[16,8,1024]{2,1,0:T(8,128)(2,1)} %bitcast.8, bf16[16,8,1024]{2,1,0:T(8,128)(2,1)} %bitcast.9, ...), custom_call_target="tpu_custom_call" | custom-call | tf_op jit(solution)/shard_map/attention/pallas_call | solution.py:590
  80.0 1.0 %store.1 = (bf16[16,8,1024]{2,1,0:T(8,128)(2,1)}, bf16[16,8,1024]{2,1,0:T(8,128)(2,1)}, bf16[16,8,1024]{2,1,0:T(8,128)(2,1)}, bf16[16,8,1024]{2,1,0:T(8,128)(2,1)}, bf16[8,1024]{1,0:T(8,128)(2,1)}) custom-call(bf16[16,8,1024]{2,1,0:T(8,128)(2,1)S(1)} %get-tuple-element.15.refs_0_, bf16[16,8,1024]{2,1,0:T(8,128)(2,1)S(1)} %get-tuple-element.16.refs_1_, ...), custom_call_target="tpu_custom_call" | custom-call | tf_op jit(solution)/shard_map/store/pallas_call | solution.py:609

commit v5 on v4

--- a/solution.py
+++ b/solution.py
@@ -258,11 +258,11 @@
             kept[pair] = probs
             target[0, :, :, lanes] = blocks(out.astype(BF16))
 
-        def two(index):
-            step(first + index * 2)
-            step(first + index * 2 + 1)
-
-        each(0, count // 2, two)
+        def four(index):
+            for part in range(4):
+                step(first + index * 4 + part)
+
+        each(0, count // 4, four)
 
     def grad_rows(source, target, first=0, parts=4):
         cotangent = flat(source[3])
@@ -278,11 +278,11 @@
             for index, term in enumerate(grads):
                 target[1 + index, :, :, lanes] = blocks(term.astype(BF16))
 
-        def two(index):
-            step(first + index * 2)
-            step(first + index * 2 + 1)
-
-        each(0, count // 2, two)
+        def four(index):
+            for part in range(4):
+                step(first + index * 4 + part)
+
+        each(0, count // 4, four)
 
     with jax.named_scope("spatial_forward"):
         forward(own, own_res, own_probs, None, 0, PAIRS // 2)
@@ -430,12 +430,10 @@
     gradient_to_chips(0)
 
     frame_forward(1)
-    with jax.named_scope("return_frame_out"):
-        return_frame(1, 0, 1, 7)
     gradient_to_chips(1)
     frame_backward(1)
     with jax.named_scope("return_frame"):
-        return_frame(1, 1, 2, 14)
+        return_frame(1, 0, 3, 7)
 
     with jax.named_scope("view_backward"):
         grad_rows(of_view, grad)
@@ -475,12 +473,12 @@
         each(1, 8, send_near)
         near_in[:, pl.ds(near, 1)] = near_out[:, pl.ds(near, 1)]
 
-    with jax.named_scope("return_frame"):
-        return_frame(1, 3, 1, 11)
-
     with jax.named_scope("spatial_backward"):
         grad_rows(own, grad)
         backward(own, own_res, own_probs, grad)
+    with jax.named_scope("return_frame"):
+        return_frame(1, 3, 1, 11)
+
     with jax.named_scope("wait_gradient_near"):
         gradient_near().wait_recv()
     with jax.named_scope("gradient_to_far"):
@@ -517,8 +515,7 @@
                 add_terms(index, columns_of(0, part))
 
     with jax.named_scope("wait_frame_back"):
-        frame_group(frame_res, frame_back, 0, 1, lanes_of_half(1), 7).wait_recv()
-        frame_group(frame_res, frame_back, 1, 2, lanes_of_half(1), 14).wait_recv()
+        frame_group(frame_res, frame_back, 0, 3, lanes_of_half(1), 7).wait_recv()
     with jax.named_scope("add_terms"):
         for index in range(3):
             for part in range(2):
@@ -558,8 +555,7 @@
             frame_group(own, of_frame, 0, 3, lanes_of_half(half), 3 + half).wait_send()
         frame_group(frame_res, frame_back, 0, 1, lanes_of_half(0), 6).wait_send()
         frame_group(frame_res, frame_back, 1, 3, lanes_of_half(0), 13).wait_send()
-        frame_group(frame_res, frame_back, 0, 1, lanes_of_half(1), 7).wait_send()
-        frame_group(frame_res, frame_back, 1, 2, lanes_of_half(1), 14).wait_send()
+        frame_group(frame_res, frame_back, 0, 3, lanes_of_half(1), 7).wait_send()
         frame_group(frame_res, frame_back, 3, 1, lanes_of_half(1), 11).wait_send()
         gradient_far().wait_send()
         gradient_near().wait_send()

time: 81.6 us -> 81.2 us (level)
  no operation moved by 1% of the time
where the time goes in v5:
time: 81.2 us; the launch traced here: 80.7 us
  Pallas kernels  80.1 us (99%)
    pallas_call x1, Pallas kernels, local(): pl.pallas_call(kernel, out_shape=(out, out, out, out, jax.ShapeDtypeStruc...  79 us

profile of v5, /device:TPU:1, one launch (start us, length us, event | category | flops | bytes accessed | tf_op | source)
XLA Modules:
  0.0 80.7 jit_solution(3783499514269800915)
XLA Ops:
  0.6 79.0 %attention.1 = (bf16[16,8,1024]{2,1,0:T(8,128)(2,1)S(1)}, bf16[16,8,1024]{2,1,0:T(8,128)(2,1)S(1)}, bf16[16,8,1024]{2,1,0:T(8,128)(2,1)S(1)}, bf16[16,8,1024]{2,1,0:T(8,128)(2,1)S(1)}, bf16[8,1024]{1,0:T(8,128)(2,1)S(1)}) custom-call(bf16[16,8,1024]{2,1,0:T(8,128)(2,1)} %bitcast.8, bf16[16,8,1024]{2,1,0:T(8,128)(2,1)} %bitcast.9, ...), custom_call_target="tpu_custom_call" | custom-call | tf_op jit(solution)/shard_map/attention/pallas_call | solution.py:586
  79.7 1.0 %store.1 = (bf16[16,8,1024]{2,1,0:T(8,128)(2,1)}, bf16[16,8,1024]{2,1,0:T(8,128)(2,1)}, bf16[16,8,1024]{2,1,0:T(8,128)(2,1)}, bf16[16,8,1024]{2,1,0:T(8,128)(2,1)}, bf16[8,1024]{1,0:T(8,128)(2,1)}) custom-call(bf16[16,8,1024]{2,1,0:T(8,128)(2,1)S(1)} %get-tuple-element.15.refs_0_, bf16[16,8,1024]{2,1,0:T(8,128)(2,1)S(1)} %get-tuple-element.16.refs_1_, ...), custom_call_target="tpu_custom_call" | custom-call | tf_op jit(solution)/shard_map/store/pallas_call | solution.py:605

commit v6 on v5

--- a/solution.py
+++ b/solution.py
@@ -176,8 +176,7 @@
         for step in range(1, VIEWS):
             greet({"view": view_peer(step)})
         pl.semaphore_wait(barrier, FRAMES - 1 + VIEWS - 1 + 6)
-        for load in loads:
-            load.wait()
+        loads[0].wait()
 
     columns = pl.ds(pl.multiple_of(view * 128, 128), 128)
 
@@ -239,6 +238,8 @@
     with jax.named_scope("send_first"):
         across.start()
         each(1, 8, send_weight(shard.at[:, columns], frame, 0))
+        for load in loads[1:]:
+            load.wait()
         each(1, FRAMES, send_frame_grad)
         each(1, VIEWS, send_view)
         weight[shard_rows(frame), columns] = shard[:, columns]
@@ -368,8 +369,6 @@
             forward(of_frame, frame_res, frame_probs, frame_bias, halves[half] * (PAIRS // 2), PAIRS // 2)
 
     def frame_backward(half):
-        with jax.named_scope("frame_grad"):
-            grad_rows(of_frame, frame_grad, halves[half] * HALF, 2)
         with jax.named_scope("frame_backward"):
             backward(of_frame, frame_res, frame_probs, frame_grad, halves[half] * (PAIRS // 2), PAIRS // 2)
 
@@ -422,6 +421,11 @@
     with jax.named_scope("wait_weight_core"):
         for onward in passes:
             onward.wait_recv()
+    def frame_grads(half):
+        with jax.named_scope("frame_grad"):
+            grad_rows(of_frame, frame_grad, halves[half] * HALF, 2)
+
+    frame_grads(0)
     frame_backward(0)
     with jax.named_scope("return_frame"):
         return_frame(0, 1, 3, 13)
@@ -429,6 +433,7 @@
         rows[128 * index : 128 * index + 128] = flat(source[3])
     gradient_to_chips(0)
 
+    frame_grads(1)
     frame_forward(1)
     gradient_to_chips(1)
     frame_backward(1)

time: 81.2 us -> 81.2 us (level)
  no operation moved by 1% of the time
where the time goes in v6:
time: 81.2 us; the launch traced here: 80.6 us
  Pallas kernels  80 us (99%)
    pallas_call x1, Pallas kernels, local(): pl.pallas_call(kernel, out_shape=(out, out, out, out, jax.ShapeDtypeStruc...  79 us

profile of v6, /device:TPU:1, one launch (start us, length us, event | category | flops | bytes accessed | tf_op | source)
XLA Modules:
  0.0 80.6 jit_solution(14679884195798730736)
XLA Ops:
  0.6 79.0 %attention.1 = (bf16[16,8,1024]{2,1,0:T(8,128)(2,1)S(1)}, bf16[16,8,1024]{2,1,0:T(8,128)(2,1)S(1)}, bf16[16,8,1024]{2,1,0:T(8,128)(2,1)S(1)}, bf16[16,8,1024]{2,1,0:T(8,128)(2,1)S(1)}, bf16[8,1024]{1,0:T(8,128)(2,1)S(1)}) custom-call(bf16[16,8,1024]{2,1,0:T(8,128)(2,1)} %bitcast.8, bf16[16,8,1024]{2,1,0:T(8,128)(2,1)} %bitcast.9, ...), custom_call_target="tpu_custom_call" | custom-call | tf_op jit(solution)/shard_map/attention/pallas_call | solution.py:591
  79.6 1.0 %store.1 = (bf16[16,8,1024]{2,1,0:T(8,128)(2,1)}, bf16[16,8,1024]{2,1,0:T(8,128)(2,1)}, bf16[16,8,1024]{2,1,0:T(8,128)(2,1)}, bf16[16,8,1024]{2,1,0:T(8,128)(2,1)}, bf16[8,1024]{1,0:T(8,128)(2,1)}) custom-call(bf16[16,8,1024]{2,1,0:T(8,128)(2,1)S(1)} %get-tuple-element.15.refs_0_, bf16[16,8,1024]{2,1,0:T(8,128)(2,1)S(1)} %get-tuple-element.16.refs_1_, ...), custom_call_target="tpu_custom_call" | custom-call | tf_op jit(solution)/shard_map/store/pallas_call | solution.py:610
